TPU v7x, 256 devices: a whole 4x4x8 slice. The times are simulated.
256 devices in a mesh: pts: 128 (over x, z, y), blk: 2 (over core).
Axes of the slice: x: 4, y: 4, z: 8, core: 2. Of those that a mesh axis runs over, the one named last changes fastest.
Arguments:
- basis_values: bfloat16 [512, 4096, 512], P(('pts', 'blk')), may hold values from -6 to 6
- density: bfloat16 [65536, 1536], P(('pts', 'blk')), may hold values from -0.01171875 to 0.01171875
- sig_blocks: int32 [512, 4], P(('pts', 'blk')), may hold values from 0 to 511, as said below
- grid_weights: float32 [512, 4096], P(('pts', 'blk')), may hold values from 0.002 to 0.02
- atom_of: int32 [512, 4096], P(('pts', 'blk')), may hold values from 0 to 4095, as said below
- in_weight: float32 [256], replicated, may hold values from -4 to 4
- in_bias: float32 [256], replicated, may hold values from -3 to 3
- atom_proj: bfloat16 [256, 64], replicated, may hold values from -0.375 to 0.375
- hidden_weight: bfloat16 [256, 256], replicated, may hold values from -0.375 to 0.375
- atom_in: bfloat16 [64, 256], replicated, may hold values from -0.75 to 0.75
- hidden_bias: float32 [256], replicated, may hold values from -3 to 3
- out_weight: bfloat16 [256], replicated, may hold values from -0.375 to 0.375
Outputs:
- potential: float32 [65536, 1536], P(('pts', 'blk'))
Inputs may be any that keep to these rules, and one draw needn't show every extreme that they name: `sig_blocks`: batch b lies on chip c = b // 4; its 4 blocks are distinct and lie in blocks 4 * (c - 1) to 4 * (c + 2) - 1. `atom_of`: every point of batch b, on chip c = b // 4, belongs to one of atoms 32 * (c - 1) to 32 * (c + 2) - 1.
All inputs are finite; a program needn't handle non-finite values.
Results may differ from a plain program's by a relative error of at most 0.0034.
Values may be sent and summed in bfloat16 or wider, within the bound.
No kernel may reach another device: no remote copies, remote signals or barrier semaphores. Data moves between devices by JAX's collectives and lax.ppermute only.
A program may use at most 128 MiB of HBM per device.

v0:
```python
import jax
import jax.numpy as jnp
from jax import lax
from jax.experimental import pallas as pl
from jax.experimental.pallas import tpu as pltpu
from jax.sharding import PartitionSpec as P

FB = 128
SIGB = 4
SIGF = 512
ATW = 64
HID = 256
CHIPB = 4
WINB = 12
HALF = 256
CHIPF = 512
CHIPA = 32
SEGS = 96
TILE = 2048
TRANS = 1024
MIB = 2**20
XROWS = 72

eps_atom = 0.0001
f32 = jnp.float32
bf16 = jnp.bfloat16

SMEM = pl.BlockSpec(memory_space=pltpu.SMEM)
VMEM = pl.BlockSpec(memory_space=pltpu.VMEM)
ANY = pl.BlockSpec(memory_space=pl.ANY)


def silu(v):
    h = 0.5 * v
    return h + h * jnp.tanh(h)


def block_of(i):
    return pl.ds(pl.multiple_of(i * FB, FB), FB)


def near(r, v):
    return jnp.abs(r // CHIPB - v // CHIPB) <= 1


def transpose_kernel(basis_ref, out_ref, token_ref):
    out_ref[0] = basis_ref[0].T
    token_ref[...] = jnp.zeros_like(token_ref)


def transpose_basis(basis):
    batches, points, funcs = basis.shape
    return pl.pallas_call(
        transpose_kernel,
        grid=(batches, points // TRANS),
        in_specs=[pl.BlockSpec((1, TRANS, funcs), lambda b, t: (b, t, 0))],
        out_specs=[
            pl.BlockSpec((1, funcs, TRANS), lambda b, t: (b, 0, t)),
            pl.BlockSpec((16, 128), lambda b, t: (0, 0)),
        ],
        out_shape=[
            jax.ShapeDtypeStruct((batches, funcs, points), bf16),
            jax.ShapeDtypeStruct((16, 128), bf16),
        ],
        compiler_params=pltpu.CompilerParams(vmem_limit_bytes=56 * MIB),
        cost_estimate=pl.CostEstimate(
            flops=10**10, bytes_accessed=4 * basis.size, transcendentals=0
        ),
    )(basis)


def tiles_of(points, batches):
    per = points // TILE
    return [(b, pl.ds(t * TILE, TILE)) for b in range(batches) for t in range(per)]


def fetch(src, dst, tiles, sems):
    copies = [
        pltpu.make_async_copy(src.at[b, :, cols], dst.at[b, :, cols], sems.at[i])
        for i, (b, cols) in enumerate(tiles)
    ]
    return copies


def first_kernel(
    scal_ref,
    own_ref,
    sib_ref,
    side_ref,
    side_sib_ref,
    bt_hbm,
    w_ref,
    atom_ref,
    in_w_ref,
    in_b_ref,
    proj_ref,
    hid_hbm,
    sums_ref,
    bt_ref,
    hid_ref,
    sub,
    acc,
    squares,
    bt_sems,
    hid_sems,
):
    core = scal_ref[8]
    atom_start = scal_ref[9]
    batches = bt_ref.shape[0]
    tiles = tiles_of(bt_ref.shape[2], batches)
    loads = fetch(bt_hbm, bt_ref, tiles, bt_sems)
    stores = fetch(hid_ref, hid_hbm, tiles, hid_sems)
    for load in loads:
        load.start()
    sources = (
        (0, side_ref, side_sib_ref, 0, 0),
        (1, own_ref, sib_ref, 0, 0),
        (2, side_ref, side_sib_ref, 2, CHIPB),
    )

    def place(i, _):
        b, k = i // SIGB, i % SIGB
        r = scal_ref[i]
        here = (r % CHIPB) // 2 == core
        for chip, mine, other, row, first in sources:
            for ref, held in ((mine, here), (other, jnp.logical_not(here))):

                @pl.when((r // CHIPB == chip) & held)
                def _():
                    for l in range(SIGB):
                        v = scal_ref[b * SIGB + l]
                        col = jnp.clip(v - first, 0, ref.shape[1] // FB - 1)
                        block = ref[block_of(row + r % 2), block_of(col)]
                        sub[b, block_of(k), l * FB : (l + 1) * FB] = jnp.where(
                            near(r, v), block, jnp.zeros_like(block)
                        )

        return 0

    lax.fori_loop(0, batches * SIGB, place, 0)
    acc[...] = jnp.zeros_like(acc)
    squares[...] = jnp.zeros_like(squares)

    def density_at(i):
        b, cols = tiles[i]
        loads[i].wait()
        bt = bt_ref[b, :, cols]
        mixed = jnp.dot(sub[b], bt, preferred_element_type=f32)
        return jnp.sum(mixed * bt.astype(f32), axis=0, keepdims=True)

    def gather_sums(i, rho):
        b, cols = tiles[i]
        hidden = silu(rho * in_w_ref[...] + in_b_ref[...]).astype(bf16)
        hid_ref[b, :, cols] = hidden
        stores[i].start()
        w = w_ref[b : b + 1, cols]
        atom = atom_ref[b : b + 1, cols] - atom_start
        w_high = w.astype(bf16).astype(f32)
        w_low = w - w_high
        match = lax.broadcasted_iota(jnp.int32, (SEGS, TILE), 0) == atom
        zero = jnp.zeros((SEGS, TILE), f32)
        member = jnp.concatenate(
            [jnp.where(match, w_high, zero), jnp.where(match, w_low, zero)], axis=0
        ).astype(bf16)
        acc[...] += lax.dot_general(
            hidden, member, (((1,), (1,)), ((), ())), preferred_element_type=f32
        )
        part = jnp.where(match, w * w, zero)
        total = part[:, :128]
        for j in range(1, TILE // 128):
            total = total + part[:, j * 128 : (j + 1) * 128]
        squares[...] += total

    rho = density_at(0)
    for i in range(1, len(tiles)):
        later = density_at(i)
        gather_sums(i - 1, rho)
        rho = later
    gather_sums(len(tiles) - 1, rho)
    weighted = acc[:, :SEGS] + acc[:, SEGS:]
    sums = jnp.dot(
        proj_ref[...].astype(f32).T,
        weighted,
        precision=lax.Precision.HIGHEST,
        preferred_element_type=f32,
    )
    sums_ref[...] = jnp.zeros_like(sums_ref)
    sums_ref[:ATW, :SEGS] = sums
    row = jnp.sum(squares[...].T, axis=0, keepdims=True)
    sums_ref[ATW : ATW + 1, :SEGS] = row
    for store in stores:
        store.wait()


def first_pass(scal, rows, bt, w, atom, in_w, in_b, proj):
    batches, funcs, points = bt.shape
    tiles = batches * points // TILE
    return pl.pallas_call(
        first_kernel,
        in_specs=[SMEM] + [VMEM] * 4 + [ANY] + [VMEM] * 5,
        out_specs=[ANY, VMEM],
        out_shape=[
            jax.ShapeDtypeStruct((batches, HID, points), bf16),
            jax.ShapeDtypeStruct((XROWS, 128), f32),
        ],
        scratch_shapes=[
            pltpu.VMEM(bt.shape, bf16),
            pltpu.VMEM((batches, HID, points), bf16),
            pltpu.VMEM((batches, SIGF, SIGF), bf16),
            pltpu.VMEM((HID, 2 * SEGS), f32),
            pltpu.VMEM((SEGS, 128), f32),
            pltpu.SemaphoreType.DMA((tiles,)),
            pltpu.SemaphoreType.DMA((tiles,)),
        ],
        compiler_params=pltpu.CompilerParams(vmem_limit_bytes=52 * MIB),
    )(scal, *rows, bt, w, atom, in_w, in_b, proj)


def second_kernel(
    scal_ref,
    x_ref,
    l1_ref,
    l2_ref,
    r1_ref,
    r2_ref,
    atom_in_ref,
    hw_ref,
    hb_ref,
    ow_ref,
    w_ref,
    atom_ref,
    hid_hbm,
    bt_hbm,
    mats_ref,
    hid_ref,
    bt_ref,
    hw_t,
    feature,
    hid_sems,
    bt_sems,
):
    atom_start = scal_ref[9]
    tiles = tiles_of(bt_ref.shape[2], bt_ref.shape[0])
    hid_loads = fetch(hid_hbm, hid_ref, tiles, hid_sems)
    bt_loads = fetch(bt_hbm, bt_ref, tiles, bt_sems)
    for hid_load, bt_load in zip(hid_loads, bt_loads):
        hid_load.start()
        bt_load.start()

    def part(ref, start, size):
        return ref[:, start * CHIPA : (start + size) * CHIPA]

    zero = jnp.zeros((XROWS, 2 * CHIPA), f32)
    total = x_ref[:, :SEGS]
    total = total + jnp.concatenate([part(l1_ref, 1, 2), zero[:, :CHIPA]], axis=1)
    total = total + jnp.concatenate([part(l2_ref, 2, 1), zero], axis=1)
    total = total + jnp.concatenate([zero[:, :CHIPA], part(r1_ref, 0, 2)], axis=1)
    total = total + jnp.concatenate([zero, part(r2_ref, 0, 1)], axis=1)
    scaled = total[:ATW] / jnp.sqrt(total[ATW : ATW + 1] + eps_atom)
    value = jnp.dot(
        atom_in_ref[...].T, scaled.astype(bf16), preferred_element_type=f32
    )
    high = value.astype(bf16)
    low = (value - high.astype(f32)).astype(bf16)
    feature[...] = jnp.concatenate([high, low], axis=1)
    hw_t[...] = hw_ref[...].T
    mats_ref[...] = jnp.zeros_like(mats_ref)

    def weigh(i):
        b, cols = tiles[i]
        atom = atom_ref[b : b + 1, cols] - atom_start
        ids = lax.broadcasted_iota(jnp.int32, (SEGS, TILE), 0)
        match = (ids == atom).astype(f32)
        member = jnp.concatenate([match, match], axis=0).astype(bf16)
        hid_loads[i].wait()
        before = (
            jnp.dot(hw_t[...], hid_ref[b, :, cols], preferred_element_type=f32)
            + jnp.dot(feature[...], member, preferred_element_type=f32)
            + hb_ref[...]
        )
        second = silu(before).astype(bf16).astype(f32)
        point = jnp.sum(second * ow_ref[...], axis=0, keepdims=True)
        scale = w_ref[b : b + 1, cols] * point
        bt_loads[i].wait()
        return (bt_ref[b, :, cols].astype(f32) * scale).astype(bf16)

    def gram(i, weighted):
        b, cols = tiles[i]
        mats_ref[b] += lax.dot_general(
            bt_ref[b, :, cols],
            weighted,
            (((1,), (1,)), ((), ())),
            preferred_element_type=f32,
        )

    weighted = weigh(0)
    for i in range(1, len(tiles)):
        later = weigh(i)
        gram(i - 1, weighted)
        weighted = later
    gram(len(tiles) - 1, weighted)


def second_pass(scal, sums, atom_in, hw, hb, ow, w, atom, hid, bt):
    batches, funcs, points = bt.shape
    tiles = batches * points // TILE
    return pl.pallas_call(
        second_kernel,
        in_specs=[SMEM] + [VMEM] * 11 + [ANY] * 2,
        out_specs=VMEM,
        out_shape=jax.ShapeDtypeStruct((batches, SIGF, SIGF), f32),
        scratch_shapes=[
            pltpu.VMEM(hid.shape, bf16),
            pltpu.VMEM(bt.shape, bf16),
            pltpu.VMEM((HID, HID), bf16),
            pltpu.VMEM((HID, 2 * SEGS), bf16),
            pltpu.SemaphoreType.DMA((tiles,)),
            pltpu.SemaphoreType.DMA((tiles,)),
        ],
        compiler_params=pltpu.CompilerParams(vmem_limit_bytes=52 * MIB),
    )(scal, *sums, atom_in, hw, hb, ow, w, atom, hid, bt)


def side_kernel(
    scal_ref, other_ref, mats_ref, got_ref, left_ref, own_ref, right_ref, to_left, to_right
):
    core = scal_ref[8]
    to_left[...] = jnp.zeros_like(to_left)
    to_right[...] = jnp.zeros_like(to_right)
    own_ref[...] = jnp.zeros_like(own_ref)
    targets = ((0, to_left, 0), (1, own_ref, 0), (2, to_right, CHIPB))
    for blocks_ref, source in ((scal_ref, mats_ref), (other_ref, got_ref)):

        def place(i, _):
            b, k = i // SIGB, i % SIGB
            r = blocks_ref[i]
            here = (r % CHIPB) // 2 == core
            for chip, ref, first in targets:

                @pl.when((r // CHIPB == chip) & here)
                def _():
                    rows = block_of(r % 2)
                    for l in range(SIGB):
                        v = blocks_ref[b * SIGB + l]
                        cols = block_of(jnp.clip(v - first, 0, ref.shape[1] // FB - 1))
                        block = source[b, block_of(k), l * FB : (l + 1) * FB]
                        ref[rows, cols] = ref[rows, cols] + jnp.where(
                            near(r, v), block, jnp.zeros_like(block)
                        )

            return 0

        lax.fori_loop(0, source.shape[0] * SIGB, place, 0)
    left_ref[...] = to_left[...].astype(bf16)
    right_ref[...] = to_right[...].astype(bf16)


def side_sums(scal, other, mats, got):
    side = jax.ShapeDtypeStruct((HALF, 2 * CHIPF), bf16)
    return pl.pallas_call(
        side_kernel,
        in_specs=[SMEM, SMEM, VMEM, VMEM],
        out_specs=[VMEM] * 3,
        out_shape=[side, jax.ShapeDtypeStruct((HALF, 3 * CHIPF), f32), side],
        scratch_shapes=[pltpu.VMEM((HALF, 2 * CHIPF), f32)] * 2,
        compiler_params=pltpu.CompilerParams(vmem_limit_bytes=20 * MIB),
    )(scal, other, mats, got)


def final_kernel(own_ref, left_ref, right_ref, out_ref):
    chip = CHIPF
    out_ref[:, :chip] = own_ref[:, :chip] + left_ref[:, :chip].astype(f32)
    out_ref[:, chip : 2 * chip] = (
        own_ref[:, chip : 2 * chip]
        + left_ref[:, chip:].astype(f32)
        + right_ref[:, :chip].astype(f32)
    )
    out_ref[:, 2 * chip :] = own_ref[:, 2 * chip :] + right_ref[:, chip:].astype(f32)


def final_sum(own, left, right):
    rows, cols = own.shape
    strip = 64
    wide = pl.BlockSpec((strip, cols), lambda i: (i, 0))
    side = pl.BlockSpec((strip, 2 * CHIPF), lambda i: (i, 0))
    return pl.pallas_call(
        final_kernel,
        grid=(rows // strip,),
        in_specs=[wide, side, side],
        out_specs=wide,
        out_shape=jax.ShapeDtypeStruct((rows, cols), f32),
        compiler_params=pltpu.CompilerParams(vmem_limit_bytes=12 * MIB),
    )(own, left, right)


def on_device(
    basis_values,
    density,
    sig_blocks,
    grid_weights,
    atom_of,
    in_weight,
    in_bias,
    atom_proj,
    hidden_weight,
    atom_in,
    hidden_bias,
    out_weight,
):
    chips = lax.axis_size("pts")
    chip = lax.axis_index("pts")
    core = lax.axis_index("blk")

    def shift(x, by):
        return lax.ppermute(x, "pts", [(i, (i + by) % chips) for i in range(chips)])

    def swap(x):
        return lax.ppermute(x, "blk", [(0, 1), (1, 0)])

    scal = jnp.concatenate(
        [
            (sig_blocks - CHIPB * (chip - 1)).reshape(-1),
            core[None].astype(jnp.int32),
            (CHIPA * (chip - 1))[None].astype(jnp.int32),
        ]
    )
    from_left = shift(density[:, CHIPF:], 1)
    from_right = shift(density[:, : 2 * CHIPF], -1)
    sibling = swap(density)
    other = swap(scal)
    bt, token = transpose_basis(basis_values)
    side = jnp.concatenate([from_left, from_right], axis=0) + token[0, 0]
    side_sib = swap(side)

    column = lambda x: x.astype(f32).reshape(HID, 1)
    hidden, sums = first_pass(
        scal,
        (density, sibling, side, side_sib),
        bt,
        grid_weights,
        atom_of,
        column(in_weight),
        column(in_bias),
        atom_proj,
    )
    sums = sums + swap(sums)
    near_sums = [shift(sums, by) for by in (1, 2, -1, -2)]
    mats = second_pass(
        scal,
        [sums] + near_sums,
        atom_in,
        hidden_weight,
        column(hidden_bias),
        column(out_weight),
        grid_weights,
        atom_of,
        hidden,
        bt,
    )
    to_left, own, to_right = side_sums(scal, other, mats, swap(mats))
    return final_sum(own, shift(to_right, 1), shift(to_left, -1))


def solution(mesh):
    return jax.shard_map(
        on_device,
        mesh=mesh,
        in_specs=(
            P(("pts", "blk"), None, None),
            P(("pts", "blk"), None),
            P(("pts", "blk"), None),
            P(("pts", "blk"), None),
            P(("pts", "blk"), None),
            P(),
            P(),
            P(),
            P(),
            P(),
            P(),
            P(),
        ),
        out_specs=P(("pts", "blk"), None),
        check_vma=False,
    )
```

profile of v0, /device:TPU:1, one launch (start us, length us, event | category | flops | bytes accessed | tf_op | source)
XLA Modules:
  0.0 99.0 jit_solution(2433891788841757176)
XLA Ops:
  0.0 1.3 %fusion = (bf16[256,1024]{1,0:T(8,128)(2,1)S(1)}, bf16[256,1024]{1,0:T(8,128)(2,1)S(1)}) fusion(bf16[256,1536]{1,0:T(8,128)(2,1)} %own_ref.1), kind=kLoop, calls=%fused_computation.3 | loop fusion | bytes 2097152 | tf_op jit(solution)/shard_map/slice | solution.py:427
  1.3 2.2 %collective-permute-start.2 = (bf16[256,1024]{1,0:T(8,128)(2,1)S(1)}, bf16[256,1024]{1,0:T(8,128)(2,1)S(1)}, u32[]{:S(2)}, u32[]{:S(2)}) collective-permute-start(bf16[256,1024]{1,0:T(8,128)(2,1)S(1)} %get-tuple-element.19), channel_id=1, source_target_pairs={{0,2},{2,4},{4,6},{6,8},{8,10},{10,12},{12,14},{14,16},{16,18},{18... | collective-permute-start | bytes 1572872 | tf_op jit(solution)/shard_map/ppermute | solution.py:415
  3.5 9.0 %collective-permute-start.3 = (bf16[256,1024]{1,0:T(8,128)(2,1)S(1)}, bf16[256,1024]{1,0:T(8,128)(2,1)S(1)}, u32[]{:S(2)}, u32[]{:S(2)}) collective-permute-start(bf16[256,1024]{1,0:T(8,128)(2,1)S(1)} %get-tuple-element.20), channel_id=1, source_target_pairs={{0,254},{2,0},{4,2},{6,4},{8,6},{10,8},{12,10},{14,12},{16,14},{18... | collective-permute-start | bytes 1572872 | tf_op jit(solution)/shard_map/ppermute | solution.py:415
  12.5 10.0 %shard_map.118 = (bf16[2,512,4096]{2,1,0:T(8,128)(2,1)}, bf16[16,128]{1,0:T(8,128)(2,1)}) custom-call(bf16[2,4096,512]{2,1,0:T(8,128)(2,1)} %basis_ref.1), custom_call_target="tpu_custom_call" | custom-call | flops 10000000000 | bytes 16777216 | tf_op jit(solution)/shard_map/pallas_call | solution.py:53
  22.6 1.3 %slice.11 = bf16[1,1]{1,0:T(2,128)(2,1)} slice(bf16[16,128]{1,0:T(8,128)(2,1)} %get-tuple-element.12), slice={[0:1], [0:1]} | slice | bytes 4 | tf_op jit(solution)/shard_map/slice | solution.py:432
  24.1 0.9 maximum_add_fusion.side_ref
  25.0 1.3 %collective-permute-start.4 = (bf16[512,1024]{1,0:T(8,128)(2,1)S(1)}, bf16[512,1024]{1,0:T(8,128)(2,1)}, u32[]{:S(2)}, u32[]{:S(2)}) collective-permute-start(bf16[512,1024]{1,0:T(8,128)(2,1)S(1)} %maximum_add_fusion.side_ref), channel_id=1, source_target_pairs={{0,1},{1,0},{2,3},{3,2},{4,5},{5,4},{6,7},{7,6},{8,9},{9,8},{10,11... | collective-permute-start | bytes 3145736 | tf_op jit(solution)/shard_map/ppermute | solution.py:418
  27.0 2.7 %collective-permute-done.1.sib_ref = bf16[256,1536]{1,0:T(8,128)(2,1)S(1)} collective-permute-done((bf16[256,1536]{1,0:T(8,128)(2,1)S(1)}, bf16[256,1536]{1,0:T(8,128)(2,1)S(1)}, u32[]{:S(2)}, u32[]{:S(2)}) %collective-permute-start.1) | collective-permute-done | bytes 786464 | tf_op jit(solution)/shard_map/ppermute | solution.py:418
  29.8 12.0 %shard_map.119 = (bf16[2,256,4096]{2,1,0:T(8,128)(2,1)}, f32[72,128]{1,0:T(8,128)S(1)}) custom-call(s32[10]{0:T(128)S(1)} %pad_add_fusion.scal_ref, bf16[256,1536]{1,0:T(8,128)(2,1)S(1)} %copy-done.1, bf16[256,1536]{1,0:T(8,128)(2,1)S(1)} %collective-permute-done.1.sib_ref, bf16[512,1024]{1,0:T(8,128)(2,1)} %copy-done.6, ...), custom_call_target="tpu_custom_call" | custom-call | tf_op jit(solution)/shard_map/pallas_call | solution.py:198
  41.8 0.5 collective-permute-start.5
  42.3 0.9 collective-permute-done.5
  43.3 7.1 %collective-permute-start.8 = (f32[72,128]{1,0:T(8,128)S(1)}, f32[72,128]{1,0:T(8,128)S(1)}, u32[]{:S(2)}, u32[]{:S(2)}) collective-permute-start(f32[72,128]{1,0:T(8,128)S(1)} %add.12.x_ref), channel_id=1, source_target_pairs={{0,254},{2,0},{4,2},{6,4},{8,6},{10,8},{12,10},{14,12},{16,14},{18... | collective-permute-start | bytes 110600 | tf_op jit(solution)/shard_map/ppermute | solution.py:415
  50.3 2.3 %collective-permute-start.9 = (f32[72,128]{1,0:T(8,128)S(1)}, f32[72,128]{1,0:T(8,128)S(1)}, u32[]{:S(2)}, u32[]{:S(2)}) collective-permute-start(f32[72,128]{1,0:T(8,128)S(1)} %add.12.x_ref), channel_id=1, source_target_pairs={{0,252},{2,254},{4,0},{6,2},{8,4},{10,6},{12,8},{14,10},{16,12},{1... | collective-permute-start | bytes 110600 | tf_op jit(solution)/shard_map/ppermute | solution.py:415
  52.9 1.7 %collective-permute-done.9.r2_ref = f32[72,128]{1,0:T(8,128)S(1)} collective-permute-done((f32[72,128]{1,0:T(8,128)S(1)}, f32[72,128]{1,0:T(8,128)S(1)}, u32[]{:S(2)}, u32[]{:S(2)}) %collective-permute-start.9) | collective-permute-done | bytes 36896 | tf_op jit(solution)/shard_map/ppermute | solution.py:415
  54.6 14.8 %shard_map.120.mats_ref = f32[2,512,512]{2,1,0:T(8,128)} custom-call(s32[10]{0:T(128)S(1)} %pad_add_fusion.scal_ref, f32[72,128]{1,0:T(8,128)S(1)} %add.12.x_ref, f32[72,128]{1,0:T(8,128)S(1)} %collective-permute-done.6.l1_ref, f32[72,128]{1,0:T(8,128)S(1)} %collective-permute-done.7.l2_ref, f32[72,128]{1,0:T(8,128)S(1)} %collective-permute-done.8.r1_ref, ...), custom_call_target="tpu_custom_call" | custom-call | tf_op jit(solution)/shard_map/pallas_call | solution.py:307
  69.4 1.9 %collective-permute-start.10 = (f32[2,512,512]{2,1,0:T(8,128)}, f32[2,512,512]{2,1,0:T(8,128)S(1)}, u32[]{:S(2)}, u32[]{:S(2)}) collective-permute-start(f32[2,512,512]{2,1,0:T(8,128)} %shard_map.120.mats_ref), channel_id=1, source_target_pairs={{0,1},{1,0},{2,3},{3,2},{4,5},{5,4},{6,7},{7,6},{8,9},{9,8},{10,11... | collective-permute-start | bytes 6291464 | tf_op jit(solution)/shard_map/ppermute | solution.py:418
  71.3 0.4 collective-permute-start
  71.7 3.4 %collective-permute-done.other_ref = s32[10]{0:T(128)S(1)} collective-permute-done((s32[10]{0:T(128)S(1)}, s32[10]{0:T(128)S(1)}, u32[]{:S(2)}, u32[]{:S(2)}) %collective-permute-start) | collective-permute-done | bytes 72 | tf_op jit(solution)/shard_map/ppermute | solution.py:418
  75.1 0.2 collective-permute-done.10.got_ref
  75.3 1.6 %copy-done = f32[2,512,512]{2,1,0:T(8,128)S(1)} copy-done((f32[2,512,512]{2,1,0:T(8,128)S(1)}, f32[2,512,512]{2,1,0:T(8,128)}, u32[]{:S(2)}) %copy-start) | copy-done | bytes 2097176
  76.9 2.0 %shard_map.121 = (bf16[256,1024]{1,0:T(8,128)(2,1)S(1)}, f32[256,1536]{1,0:T(8,128)S(1)}, bf16[256,1024]{1,0:T(8,128)(2,1)S(1)}) custom-call(s32[10]{0:T(128)S(1)} %pad_add_fusion.scal_ref, s32[10]{0:T(128)S(1)} %collective-permute-done.other_ref, f32[2,512,512]{2,1,0:T(8,128)S(1)} %copy-done, f32[2,512,512]{2,1,0:T(8,128)S(1)} %collective-permute-done.10.got_ref), custom_call_target="tpu_custom_call" | custom-call | tf_op jit(solution)/shard_map/pallas_call | solution.py:360
  79.0 6.9 %collective-permute-start.12 = (bf16[256,1024]{1,0:T(8,128)(2,1)S(1)}, bf16[256,1024]{1,0:T(8,128)(2,1)S(1)}, u32[]{:S(2)}, u32[]{:S(2)}) collective-permute-start(bf16[256,1024]{1,0:T(8,128)(2,1)S(1)} %get-tuple-element.18), channel_id=1, source_target_pairs={{0,254},{2,0},{4,2},{6,4},{8,6},{10,8},{12,10},{14,12},{16,14},{18... | collective-permute-start | bytes 1572872 | tf_op jit(solution)/shard_map/ppermute | solution.py:415
  85.9 11.5 %collective-permute-done.11.left_ref = bf16[256,1024]{1,0:T(8,128)(2,1)S(1)} collective-permute-done((bf16[256,1024]{1,0:T(8,128)(2,1)S(1)}, bf16[256,1024]{1,0:T(8,128)(2,1)S(1)}, u32[]{:S(2)}, u32[]{:S(2)}) %collective-permute-start.11) | collective-permute-done | bytes 524320 | tf_op jit(solution)/shard_map/ppermute | solution.py:415
  97.3 1.7 %shard_map.122 = f32[256,1536]{1,0:T(8,128)} custom-call(f32[256,1536]{1,0:T(8,128)S(1)} %get-tuple-element.16.own_ref, bf16[256,1024]{1,0:T(8,128)(2,1)S(1)} %collective-permute-done.11.left_ref, bf16[256,1024]{1,0:T(8,128)(2,1)S(1)} %collective-permute-done.12.right_ref), custom_call_target="tpu_custom_call" | custom-call | tf_op jit(solution)/shard_map/pallas_call | solution.py:386
  (46 shorter events, 1.3 us)
Async XLA Ops:
  1.3 22.8 %collective-permute-start.2 = (bf16[256,1024]{1,0:T(8,128)(2,1)S(1)}, bf16[256,1024]{1,0:T(8,128)(2,1)S(1)}, u32[]{:S(2)}, u32[]{:S(2)}) collective-permute-start(bf16[256,1024]{1,0:T(8,128)(2,1)S(1)} %get-tuple-element.19), channel_id=1, source_target_pairs={{0,2},{2,4},{4,6},{6,8},{8,10},{10,12},{12,14},{14,16},{16,18},{18... | collective-permute-start | bytes 1572872 | tf_op jit(solution)/shard_map/ppermute | solution.py:415
  3.5 20.6 %collective-permute-start.3 = (bf16[256,1024]{1,0:T(8,128)(2,1)S(1)}, bf16[256,1024]{1,0:T(8,128)(2,1)S(1)}, u32[]{:S(2)}, u32[]{:S(2)}) collective-permute-start(bf16[256,1024]{1,0:T(8,128)(2,1)S(1)} %get-tuple-element.20), channel_id=1, source_target_pairs={{0,254},{2,0},{4,2},{6,4},{8,6},{10,8},{12,10},{14,12},{16,14},{18... | collective-permute-start | bytes 1572872 | tf_op jit(solution)/shard_map/ppermute | solution.py:415
  22.6 3.9 %copy-start.11 = (s32[2,4]{1,0:T(2,128)S(1)}, s32[2,4]{1,0:T(2,128)}, u32[]{:S(2)}) copy-start(s32[2,4]{1,0:T(2,128)} %param.14) | copy-start | bytes 100
  22.6 4.0 %copy-start.8 = (f32[256]{0:T(256)S(1)}, f32[256]{0:T(256)}, u32[]{:S(2)}) copy-start(f32[256]{0:T(256)} %param.17) | copy-start | bytes 3076
  22.6 4.1 %copy-start.9 = (f32[256]{0:T(256)S(1)}, f32[256]{0:T(256)}, u32[]{:S(2)}) copy-start(f32[256]{0:T(256)} %param.18) | copy-start | bytes 3076
  22.6 4.2 %copy-start.7 = (bf16[256,64]{0,1:T(8,128)(2,1)S(1)}, bf16[256,64]{0,1:T(8,128)(2,1)}, u32[]{:S(2)}) copy-start(bf16[256,64]{0,1:T(8,128)(2,1)} %param.19) | copy-start | bytes 98308
  22.6 7.1 %copy-start.3 = (f32[2,4096]{1,0:T(2,128)S(1)}, f32[2,4096]{1,0:T(2,128)}, u32[]{:S(2)}) copy-start(f32[2,4096]{1,0:T(2,128)} %w_ref.3) | copy-start | bytes 98308
  22.6 7.1 %copy-start.4 = (s32[2,4096]{1,0:T(2,128)S(1)}, s32[2,4096]{1,0:T(2,128)}, u32[]{:S(2)}) copy-start(s32[2,4096]{1,0:T(2,128)} %atom_ref.3) | copy-start | bytes 98308
  25.0 4.7 %copy-start.6 = (bf16[512,1024]{1,0:T(8,128)(2,1)}, bf16[512,1024]{1,0:T(8,128)(2,1)S(1)}, u32[]{:S(2)}) copy-start(bf16[512,1024]{1,0:T(8,128)(2,1)S(1)} %maximum_add_fusion.side_ref) | copy-start | bytes 3145732
  25.0 4.7 %collective-permute-start.4 = (bf16[512,1024]{1,0:T(8,128)(2,1)S(1)}, bf16[512,1024]{1,0:T(8,128)(2,1)}, u32[]{:S(2)}, u32[]{:S(2)}) collective-permute-start(bf16[512,1024]{1,0:T(8,128)(2,1)S(1)} %maximum_add_fusion.side_ref), channel_id=1, source_target_pairs={{0,1},{1,0},{2,3},{3,2},{4,5},{5,4},{6,7},{7,6},{8,9},{9,8},{10,11... | collective-permute-start | bytes 3145736 | tf_op jit(solution)/shard_map/ppermute | solution.py:418
  26.3 3.4 %collective-permute-start.1 = (bf16[256,1536]{1,0:T(8,128)(2,1)S(1)}, bf16[256,1536]{1,0:T(8,128)(2,1)S(1)}, u32[]{:S(2)}, u32[]{:S(2)}) collective-permute-start(bf16[256,1536]{1,0:T(8,128)(2,1)S(1)} %copy-done.1), channel_id=1, source_target_pairs={{0,1},{1,0},{2,3},{3,2},{4,5},{5,4},{6,7},{7,6},{8,9},{9,8},{10,11... | collective-permute-start | bytes 2359304 | tf_op jit(solution)/shard_map/ppermute | solution.py:418
  29.8 22.8 %copy-start.12 = (bf16[256]{0:T(256)(128)(2,1)S(1)}, bf16[256]{0:T(256)(128)(2,1)}, u32[]{:S(2)}) copy-start(bf16[256]{0:T(256)(128)(2,1)} %param.23) | copy-start | bytes 1540
  29.8 23.0 %copy-start.10 = (f32[256]{0:T(256)S(1)}, f32[256]{0:T(256)}, u32[]{:S(2)}) copy-start(f32[256]{0:T(256)} %param.22) | copy-start | bytes 3076
  29.8 24.9 %copy-start.2 = (bf16[256,256]{1,0:T(8,128)(2,1)S(1)}, bf16[256,256]{1,0:T(8,128)(2,1)}, u32[]{:S(2)}) copy-start(bf16[256,256]{1,0:T(8,128)(2,1)} %hw_ref.1) | copy-start | bytes 393220
  29.8 24.8 %copy-start.5 = (bf16[64,256]{1,0:T(8,128)(2,1)S(1)}, bf16[64,256]{1,0:T(8,128)(2,1)}, u32[]{:S(2)}) copy-start(bf16[64,256]{1,0:T(8,128)(2,1)} %atom_in_ref.1) | copy-start | bytes 98308
  41.8 1.3 %collective-permute-start.5 = (f32[72,128]{1,0:T(8,128)S(1)}, f32[72,128]{1,0:T(8,128)S(1)}, u32[]{:S(2)}, u32[]{:S(2)}) collective-permute-start(f32[72,128]{1,0:T(8,128)S(1)} %get-tuple-element.14), channel_id=1, source_target_pairs={{0,1},{1,0},{2,3},{3,2},{4,5},{5,4},{6,7},{7,6},{8,9},{9,8},{10,11... | collective-permute-start | bytes 110600 | tf_op jit(solution)/shard_map/ppermute | solution.py:418
  43.2 9.7 %collective-permute-start.6 = (f32[72,128]{1,0:T(8,128)S(1)}, f32[72,128]{1,0:T(8,128)S(1)}, u32[]{:S(2)}, u32[]{:S(2)}) collective-permute-start(f32[72,128]{1,0:T(8,128)S(1)} %add.12.x_ref), channel_id=1, source_target_pairs={{0,2},{2,4},{4,6},{6,8},{8,10},{10,12},{12,14},{14,16},{16,18},{18... | collective-permute-start | bytes 110600 | tf_op jit(solution)/shard_map/ppermute | solution.py:415
  43.2 9.7 %collective-permute-start.7 = (f32[72,128]{1,0:T(8,128)S(1)}, f32[72,128]{1,0:T(8,128)S(1)}, u32[]{:S(2)}, u32[]{:S(2)}) collective-permute-start(f32[72,128]{1,0:T(8,128)S(1)} %add.12.x_ref), channel_id=1, source_target_pairs={{0,4},{2,6},{4,8},{6,10},{8,12},{10,14},{12,16},{14,18},{16,20},{1... | collective-permute-start | bytes 110600 | tf_op jit(solution)/shard_map/ppermute | solution.py:415
  43.3 9.7 %collective-permute-start.8 = (f32[72,128]{1,0:T(8,128)S(1)}, f32[72,128]{1,0:T(8,128)S(1)}, u32[]{:S(2)}, u32[]{:S(2)}) collective-permute-start(f32[72,128]{1,0:T(8,128)S(1)} %add.12.x_ref), channel_id=1, source_target_pairs={{0,254},{2,0},{4,2},{6,4},{8,6},{10,8},{12,10},{14,12},{16,14},{18... | collective-permute-start | bytes 110600 | tf_op jit(solution)/shard_map/ppermute | solution.py:415
  50.3 4.3 %collective-permute-start.9 = (f32[72,128]{1,0:T(8,128)S(1)}, f32[72,128]{1,0:T(8,128)S(1)}, u32[]{:S(2)}, u32[]{:S(2)}) collective-permute-start(f32[72,128]{1,0:T(8,128)S(1)} %add.12.x_ref), channel_id=1, source_target_pairs={{0,252},{2,254},{4,0},{6,2},{8,4},{10,6},{12,8},{14,10},{16,12},{1... | collective-permute-start | bytes 110600 | tf_op jit(solution)/shard_map/ppermute | solution.py:415
  69.4 5.9 %collective-permute-start.10 = (f32[2,512,512]{2,1,0:T(8,128)}, f32[2,512,512]{2,1,0:T(8,128)S(1)}, u32[]{:S(2)}, u32[]{:S(2)}) collective-permute-start(f32[2,512,512]{2,1,0:T(8,128)} %shard_map.120.mats_ref), channel_id=1, source_target_pairs={{0,1},{1,0},{2,3},{3,2},{4,5},{5,4},{6,7},{7,6},{8,9},{9,8},{10,11... | collective-permute-start | bytes 6291464 | tf_op jit(solution)/shard_map/ppermute | solution.py:418
  71.3 3.8 %collective-permute-start = (s32[10]{0:T(128)S(1)}, s32[10]{0:T(128)S(1)}, u32[]{:S(2)}, u32[]{:S(2)}) collective-permute-start(s32[10]{0:T(128)S(1)} %pad_add_fusion.scal_ref), channel_id=1, source_target_pairs={{0,1},{1,0},{2,3},{3,2},{4,5},{5,4},{6,7},{7,6},{8,9},{9,8},{10,11... | collective-permute-start | bytes 128 | tf_op jit(solution)/shard_map/ppermute | solution.py:418
  78.9 18.5 %collective-permute-start.11 = (bf16[256,1024]{1,0:T(8,128)(2,1)S(1)}, bf16[256,1024]{1,0:T(8,128)(2,1)S(1)}, u32[]{:S(2)}, u32[]{:S(2)}) collective-permute-start(bf16[256,1024]{1,0:T(8,128)(2,1)S(1)} %get-tuple-element.17), channel_id=1, source_target_pairs={{0,2},{2,4},{4,6},{6,8},{8,10},{10,12},{12,14},{14,16},{16,18},{18... | collective-permute-start | bytes 1572872 | tf_op jit(solution)/shard_map/ppermute | solution.py:415
  79.0 18.4 %collective-permute-start.12 = (bf16[256,1024]{1,0:T(8,128)(2,1)S(1)}, bf16[256,1024]{1,0:T(8,128)(2,1)S(1)}, u32[]{:S(2)}, u32[]{:S(2)}) collective-permute-start(bf16[256,1024]{1,0:T(8,128)(2,1)S(1)} %get-tuple-element.18), channel_id=1, source_target_pairs={{0,254},{2,0},{4,2},{6,4},{8,6},{10,8},{12,10},{14,12},{16,14},{18... | collective-permute-start | bytes 1572872 | tf_op jit(solution)/shard_map/ppermute | solution.py:415
  (2 other events, 5.3 us)
where the time goes:
time: 99.8 us; the launch traced here: 99 us
  Pallas kernels  40.5 us (41%)
  starting transfers between devices  31.7 us (32%)
  waiting for transfers between devices  20.5 us (21%)
  local copies, waits for them, and re-layouts  5.03 us (5%)
    ppermute x8, starting transfers between devices, shift(): return lax.ppermute(x, 'pts', [(i, (i + by) % chips) for i in range(chips)])  27.6 us
    pallas_call x1, Pallas kernels, second_pass(): pl.pallas_call(second_kernel, in_specs=[SMEM] + [VMEM] * 11 + [ANY] * 2,...  14.8 us
    ppermute x8, waiting for transfers between devices, shift(): return lax.ppermute(x, 'pts', [(i, (i + by) % chips) for i in range(chips)])  13.3 us
    pallas_call x1, Pallas kernels, first_pass(): pl.pallas_call(first_kernel, in_specs=[SMEM] + [VMEM] * 4 + [ANY] + [VMEM...  12 us
    pallas_call x1, Pallas kernels, transpose_basis(): pl.pallas_call(transpose_kernel, grid=(batches, points // TRANS), in_spec...  10 us
    ppermute x5, waiting for transfers between devices, swap(): return lax.ppermute(x, 'blk', [(0, 1), (1, 0)])  7.21 us
    ppermute x5, starting transfers between devices, swap(): return lax.ppermute(x, 'blk', [(0, 1), (1, 0)])  4.12 us
  transfers between devices with their start and end apart: 13, of which 7 were waited for; matrix products, arithmetic and copies ran while one was open for 2% of the time, Pallas kernels for 10%

commit v1 on v0

--- a/solution.py
+++ b/solution.py
@@ -30,9 +30,8 @@
 ANY = pl.BlockSpec(memory_space=pl.ANY)
 
 
-def silu(v):
-    h = 0.5 * v
-    return h + h * jnp.tanh(h)
+def silu_of_twice(h):
+    return h * (1.0 + jnp.tanh(h))
 
 
 def block_of(i):
@@ -150,7 +149,7 @@
 
     def gather_sums(i, rho):
         b, cols = tiles[i]
-        hidden = silu(rho * in_w_ref[...] + in_b_ref[...]).astype(bf16)
+        hidden = silu_of_twice(rho * in_w_ref[...] + in_b_ref[...]).astype(bf16)
         hid_ref[b, :, cols] = hidden
         stores[i].start()
         w = w_ref[b : b + 1, cols]
@@ -171,12 +170,8 @@
             total = total + part[:, j * 128 : (j + 1) * 128]
         squares[...] += total
 
-    rho = density_at(0)
-    for i in range(1, len(tiles)):
-        later = density_at(i)
-        gather_sums(i - 1, rho)
-        rho = later
-    gather_sums(len(tiles) - 1, rho)
+    for i in range(len(tiles)):
+        gather_sums(i, density_at(i))
     weighted = acc[:, :SEGS] + acc[:, SEGS:]
     sums = jnp.dot(
         proj_ref[...].astype(f32).T,
@@ -216,15 +211,39 @@
     )(scal, *rows, bt, w, atom, in_w, in_b, proj)
 
 
+def layer_kernel(hw_ref, hid_ref, out_ref, hw_t):
+    @pl.when((pl.program_id(0) == 0) & (pl.program_id(1) == 0))
+    def _():
+        hw_t[...] = (0.5 * hw_ref[...].astype(f32)).T.astype(bf16)
+
+    out_ref[0] = jnp.dot(hw_t[...], hid_ref[0], preferred_element_type=f32)
+
+
+def layer(hw, hid):
+    batches, units, points = hid.shape
+    spec = pl.BlockSpec((1, units, TILE), lambda b, t: (b, 0, t))
+    return pl.pallas_call(
+        layer_kernel,
+        grid=(batches, points // TILE),
+        in_specs=[pl.BlockSpec((units, units), lambda b, t: (0, 0)), spec],
+        out_specs=spec,
+        out_shape=jax.ShapeDtypeStruct(hid.shape, f32),
+        scratch_shapes=[pltpu.VMEM((units, units), bf16)],
+        compiler_params=pltpu.CompilerParams(vmem_limit_bytes=52 * MIB),
+        cost_estimate=pl.CostEstimate(
+            flops=10**10, bytes_accessed=6 * hid.size, transcendentals=0
+        ),
+    )(hw, hid)
+
+
 def second_kernel(
     scal_ref,
     x_ref,
-    l1_ref,
-    l2_ref,
-    r1_ref,
-    r2_ref,
+    even_ref,
+    odd_ref,
+    even2_ref,
+    odd2_ref,
     atom_in_ref,
-    hw_ref,
     hb_ref,
     ow_ref,
     w_ref,
@@ -232,9 +251,9 @@
     hid_hbm,
     bt_hbm,
     mats_ref,
+    send_ref,
     hid_ref,
     bt_ref,
-    hw_t,
     feature,
     hid_sems,
     bt_sems,
@@ -247,23 +266,30 @@
         hid_load.start()
         bt_load.start()
 
-    def part(ref, start, size):
-        return ref[:, start * CHIPA : (start + size) * CHIPA]
+    first = scal_ref[10] == 0
+    first2 = scal_ref[11] == 0
+    left1 = jnp.where(first, odd_ref[...], even_ref[...])
+    right1 = jnp.where(first, even_ref[...], odd_ref[...])
+    left2 = jnp.where(first2, odd2_ref[...], even2_ref[...])
+    right2 = jnp.where(first2, even2_ref[...], odd2_ref[...])
+
+    def part(x, start, size):
+        return x[:, start * CHIPA : (start + size) * CHIPA]
 
     zero = jnp.zeros((XROWS, 2 * CHIPA), f32)
     total = x_ref[:, :SEGS]
-    total = total + jnp.concatenate([part(l1_ref, 1, 2), zero[:, :CHIPA]], axis=1)
-    total = total + jnp.concatenate([part(l2_ref, 2, 1), zero], axis=1)
-    total = total + jnp.concatenate([zero[:, :CHIPA], part(r1_ref, 0, 2)], axis=1)
-    total = total + jnp.concatenate([zero, part(r2_ref, 0, 1)], axis=1)
+    total = total + jnp.concatenate([part(left1, 1, 2), zero[:, :CHIPA]], axis=1)
+    total = total + jnp.concatenate([part(left2, 2, 1), zero], axis=1)
+    total = total + jnp.concatenate([zero[:, :CHIPA], part(right1, 0, 2)], axis=1)
+    total = total + jnp.concatenate([zero, part(right2, 0, 1)], axis=1)
     scaled = total[:ATW] / jnp.sqrt(total[ATW : ATW + 1] + eps_atom)
     value = jnp.dot(
         atom_in_ref[...].T, scaled.astype(bf16), preferred_element_type=f32
     )
+    value = 0.5 * (value + hb_ref[...])
     high = value.astype(bf16)
     low = (value - high.astype(f32)).astype(bf16)
     feature[...] = jnp.concatenate([high, low], axis=1)
-    hw_t[...] = hw_ref[...].T
     mats_ref[...] = jnp.zeros_like(mats_ref)
 
     def weigh(i):
@@ -273,12 +299,10 @@
         match = (ids == atom).astype(f32)
         member = jnp.concatenate([match, match], axis=0).astype(bf16)
         hid_loads[i].wait()
-        before = (
-            jnp.dot(hw_t[...], hid_ref[b, :, cols], preferred_element_type=f32)
-            + jnp.dot(feature[...], member, preferred_element_type=f32)
-            + hb_ref[...]
+        half = hid_ref[b, :, cols] + jnp.dot(
+            feature[...], member, preferred_element_type=f32
         )
-        second = silu(before).astype(bf16).astype(f32)
+        second = silu_of_twice(half)
         point = jnp.sum(second * ow_ref[...], axis=0, keepdims=True)
         scale = w_ref[b : b + 1, cols] * point
         bt_loads[i].wait()
@@ -293,42 +317,37 @@
             preferred_element_type=f32,
         )
 
-    weighted = weigh(0)
-    for i in range(1, len(tiles)):
-        later = weigh(i)
-        gram(i - 1, weighted)
-        weighted = later
-    gram(len(tiles) - 1, weighted)
-
-
-def second_pass(scal, sums, atom_in, hw, hb, ow, w, atom, hid, bt):
+    for i in range(len(tiles)):
+        gram(i, weigh(i))
+    send_ref[...] = mats_ref[...].astype(bf16)
+
+
+def second_pass(scal, sums, atom_in, hb, ow, w, atom, hid, bt):
     batches, funcs, points = bt.shape
     tiles = batches * points // TILE
     return pl.pallas_call(
         second_kernel,
-        in_specs=[SMEM] + [VMEM] * 11 + [ANY] * 2,
-        out_specs=VMEM,
-        out_shape=jax.ShapeDtypeStruct((batches, SIGF, SIGF), f32),
+        in_specs=[SMEM] + [VMEM] * 10 + [ANY] * 2,
+        out_specs=[VMEM] * 2,
+        out_shape=[
+            jax.ShapeDtypeStruct((batches, SIGF, SIGF), f32),
+            jax.ShapeDtypeStruct((batches, SIGF, SIGF), bf16),
+        ],
         scratch_shapes=[
-            pltpu.VMEM(hid.shape, bf16),
+            pltpu.VMEM(hid.shape, f32),
             pltpu.VMEM(bt.shape, bf16),
-            pltpu.VMEM((HID, HID), bf16),
             pltpu.VMEM((HID, 2 * SEGS), bf16),
             pltpu.SemaphoreType.DMA((tiles,)),
             pltpu.SemaphoreType.DMA((tiles,)),
         ],
         compiler_params=pltpu.CompilerParams(vmem_limit_bytes=52 * MIB),
-    )(scal, *sums, atom_in, hw, hb, ow, w, atom, hid, bt)
-
-
-def side_kernel(
-    scal_ref, other_ref, mats_ref, got_ref, left_ref, own_ref, right_ref, to_left, to_right
-):
+    )(scal, *sums, atom_in, hb, ow, w, atom, hid, bt)
+
+
+def scatter(scal_ref, other_ref, mats_ref, got_ref, targets):
     core = scal_ref[8]
-    to_left[...] = jnp.zeros_like(to_left)
-    to_right[...] = jnp.zeros_like(to_right)
-    own_ref[...] = jnp.zeros_like(own_ref)
-    targets = ((0, to_left, 0), (1, own_ref, 0), (2, to_right, CHIPB))
+    for _, ref, _ in targets:
+        ref[...] = jnp.zeros_like(ref)
     for blocks_ref, source in ((scal_ref, mats_ref), (other_ref, got_ref)):
 
         def place(i, _):
@@ -343,7 +362,7 @@
                     for l in range(SIGB):
                         v = blocks_ref[b * SIGB + l]
                         cols = block_of(jnp.clip(v - first, 0, ref.shape[1] // FB - 1))
-                        block = source[b, block_of(k), l * FB : (l + 1) * FB]
+                        block = source[b, block_of(k), l * FB : (l + 1) * FB].astype(f32)
                         ref[rows, cols] = ref[rows, cols] + jnp.where(
                             near(r, v), block, jnp.zeros_like(block)
                         )
@@ -351,6 +370,13 @@
             return 0
 
         lax.fori_loop(0, source.shape[0] * SIGB, place, 0)
+
+
+def side_kernel(
+    scal_ref, other_ref, mats_ref, got_ref, left_ref, right_ref, to_left, to_right
+):
+    targets = ((0, to_left, 0), (2, to_right, CHIPB))
+    scatter(scal_ref, other_ref, mats_ref, got_ref, targets)
     left_ref[...] = to_left[...].astype(bf16)
     right_ref[...] = to_right[...].astype(bf16)
 
@@ -360,10 +386,27 @@
     return pl.pallas_call(
         side_kernel,
         in_specs=[SMEM, SMEM, VMEM, VMEM],
-        out_specs=[VMEM] * 3,
-        out_shape=[side, jax.ShapeDtypeStruct((HALF, 3 * CHIPF), f32), side],
+        out_specs=[VMEM] * 2,
+        out_shape=[side] * 2,
         scratch_shapes=[pltpu.VMEM((HALF, 2 * CHIPF), f32)] * 2,
         compiler_params=pltpu.CompilerParams(vmem_limit_bytes=20 * MIB),
+    )(scal, other, mats, got)
+
+
+def own_kernel(scal_ref, other_ref, mats_ref, got_ref, own_ref):
+    scatter(scal_ref, other_ref, mats_ref, got_ref, ((1, own_ref, 0),))
+
+
+def own_sums(scal, other, mats, got):
+    return pl.pallas_call(
+        own_kernel,
+        in_specs=[SMEM, SMEM, VMEM, VMEM],
+        out_specs=VMEM,
+        out_shape=jax.ShapeDtypeStruct((HALF, 3 * CHIPF), f32),
+        compiler_params=pltpu.CompilerParams(vmem_limit_bytes=20 * MIB),
+        cost_estimate=pl.CostEstimate(
+            flops=10**9, bytes_accessed=8 * mats.size, transcendentals=0
+        ),
     )(scal, other, mats, got)
 
 
@@ -380,7 +423,7 @@
 
 def final_sum(own, left, right):
     rows, cols = own.shape
-    strip = 64
+    strip = 128
     wide = pl.BlockSpec((strip, cols), lambda i: (i, 0))
     side = pl.BlockSpec((strip, 2 * CHIPF), lambda i: (i, 0))
     return pl.pallas_call(
@@ -414,6 +457,10 @@
     def shift(x, by):
         return lax.ppermute(x, "pts", [(i, (i + by) % chips) for i in range(chips)])
 
+    def pair(x, by, start):
+        to = lambda i: (((i - start) % chips) ^ by) + start
+        return lax.ppermute(x, "pts", [(i, to(i) % chips) for i in range(chips)])
+
     def swap(x):
         return lax.ppermute(x, "blk", [(0, 1), (1, 0)])
 
@@ -422,6 +469,8 @@
             (sig_blocks - CHIPB * (chip - 1)).reshape(-1),
             core[None].astype(jnp.int32),
             (CHIPA * (chip - 1))[None].astype(jnp.int32),
+            (chip % 2)[None].astype(jnp.int32),
+            ((chip // 2) % 2)[None].astype(jnp.int32),
         ]
     )
     from_left = shift(density[:, CHIPF:], 1)
@@ -432,32 +481,34 @@
     side = jnp.concatenate([from_left, from_right], axis=0) + token[0, 0]
     side_sib = swap(side)
 
-    column = lambda x: x.astype(f32).reshape(HID, 1)
+    column = lambda x, by=1.0: (by * x.astype(f32)).reshape(HID, 1)
     hidden, sums = first_pass(
         scal,
         (density, sibling, side, side_sib),
         bt,
         grid_weights,
         atom_of,
-        column(in_weight),
-        column(in_bias),
+        column(in_weight, 0.5),
+        column(in_bias, 0.5),
         atom_proj,
     )
     sums = sums + swap(sums)
-    near_sums = [shift(sums, by) for by in (1, 2, -1, -2)]
-    mats = second_pass(
+    near_sums = [pair(sums, by, start) for by, start in ((1, 0), (2, 0), (1, 1), (2, 2))]
+    half = layer(hidden_weight, hidden)
+    mats, send = second_pass(
         scal,
-        [sums] + near_sums,
+        [sums, near_sums[0], near_sums[2], near_sums[1], near_sums[3]],
         atom_in,
-        hidden_weight,
         column(hidden_bias),
         column(out_weight),
         grid_weights,
         atom_of,
-        hidden,
+        half,
         bt,
     )
-    to_left, own, to_right = side_sums(scal, other, mats, swap(mats))
+    got = swap(send)
+    to_left, to_right = side_sums(scal, other, mats, got)
+    own = own_sums(scal, other, mats, got)
     return final_sum(own, shift(to_right, 1), shift(to_left, -1))
 
 

time: 99.8 us -> 97 us (0.972)
  waiting for transfers between devices: 20.5 us -> 16.9 us
  Pallas kernels: 40.5 us -> 43.4 us
  starting transfers between devices: 31.7 us -> 30.2 us
    ppermute x8 -> x4, starting transfers between devices: 27.6 us -> 18.2 us  [shift(): return lax.ppermute(x, 'pts', [(i, (i + by) % chips) for i in range(chips)])]
    ppermute x0 -> x4, starting transfers between devices: none -> 8.16 us  [pair(): return lax.ppermute(x, 'pts', [(i, to(i) % chips) for i in range(chips)])]
    pallas_call x1 -> x3, Pallas kernels: 14.8 us -> 19.3 us  [the longest x1 11.3 us: second_pass(): pl.pallas_call(second_kernel, in_specs=[SMEM] + [VMEM] * 10 + [ANY] * 2,...]
    ppermute x8 -> x4, waiting for transfers between devices: 13.3 us -> 10.6 us  [shift(): return lax.ppermute(x, 'pts', [(i, (i + by) % chips) for i in range(chips)])]
    ppermute x5, waiting for transfers between devices: 7.21 us -> 5.43 us  [swap(): return lax.ppermute(x, 'blk', [(0, 1), (1, 0)])]
  transfers between devices with their start and end apart: 13 -> 13, of which waited for: 7 -> 6; matrix products, arithmetic and copies ran while one was open for 2% -> 2% of each run, Pallas kernels for 10% -> 19%
where the time goes in v1:
time: 97 us; the launch traced here: 96.5 us
  Pallas kernels  43.4 us (45%)
  starting transfers between devices  30.2 us (31%)
  waiting for transfers between devices  16.9 us (17%)
  local copies, waits for them, and re-layouts  5.01 us (5%)
    ppermute x4, starting transfers between devices, shift(): return lax.ppermute(x, 'pts', [(i, (i + by) % chips) for i in range(chips)])  18.2 us
    pallas_call x1, Pallas kernels, second_pass(): pl.pallas_call(second_kernel, in_specs=[SMEM] + [VMEM] * 10 + [ANY] * 2,...  11.3 us
    pallas_call x1, Pallas kernels, first_pass(): pl.pallas_call(first_kernel, in_specs=[SMEM] + [VMEM] * 4 + [ANY] + [VMEM...  11.3 us
    ppermute x4, waiting for transfers between devices, shift(): return lax.ppermute(x, 'pts', [(i, (i + by) % chips) for i in range(chips)])  10.6 us
    pallas_call x1, Pallas kernels, transpose_basis(): pl.pallas_call(transpose_kernel, grid=(batches, points // TRANS), in_spec...  10.1 us
    ppermute x4, starting transfers between devices, pair(): return lax.ppermute(x, 'pts', [(i, to(i) % chips) for i in range(chips)])  8.16 us
    pallas_call x1, Pallas kernels, layer(): pl.pallas_call(layer_kernel, grid=(batches, points // TILE), in_specs=[pl...  6.71 us
    ppermute x5, waiting for transfers between devices, swap(): return lax.ppermute(x, 'blk', [(0, 1), (1, 0)])  5.43 us
  transfers between devices with their start and end apart: 13, of which 6 were waited for; matrix products, arithmetic and copies ran while one was open for 2% of the time, Pallas kernels for 19%

profile of v1, /device:TPU:1, one launch (start us, length us, event | category | flops | bytes accessed | tf_op | source)
XLA Modules:
  0.0 96.5 jit_solution(17906557509061257139)
XLA Ops:
  0.0 1.3 %fusion = (bf16[256,1024]{1,0:T(8,128)(2,1)S(1)}, bf16[256,1024]{1,0:T(8,128)(2,1)S(1)}) fusion(bf16[256,1536]{1,0:T(8,128)(2,1)} %own_ref.1), kind=kLoop, calls=%fused_computation.4 | loop fusion | bytes 2097152 | tf_op jit(solution)/shard_map/slice | solution.py:476
  1.3 2.2 %collective-permute-start.2 = (bf16[256,1024]{1,0:T(8,128)(2,1)S(1)}, bf16[256,1024]{1,0:T(8,128)(2,1)S(1)}, u32[]{:S(2)}, u32[]{:S(2)}) collective-permute-start(bf16[256,1024]{1,0:T(8,128)(2,1)S(1)} %get-tuple-element.21), channel_id=1, source_target_pairs={{0,2},{2,4},{4,6},{6,8},{8,10},{10,12},{12,14},{14,16},{16,18},{18... | collective-permute-start | bytes 1572872 | tf_op jit(solution)/shard_map/ppermute | solution.py:458
  3.5 9.0 %collective-permute-start.3 = (bf16[256,1024]{1,0:T(8,128)(2,1)S(1)}, bf16[256,1024]{1,0:T(8,128)(2,1)S(1)}, u32[]{:S(2)}, u32[]{:S(2)}) collective-permute-start(bf16[256,1024]{1,0:T(8,128)(2,1)S(1)} %get-tuple-element.22), channel_id=1, source_target_pairs={{0,254},{2,0},{4,2},{6,4},{8,6},{10,8},{12,10},{14,12},{16,14},{18... | collective-permute-start | bytes 1572872 | tf_op jit(solution)/shard_map/ppermute | solution.py:458
  12.5 10.1 %shard_map.118 = (bf16[2,512,4096]{2,1,0:T(8,128)(2,1)}, bf16[16,128]{1,0:T(8,128)(2,1)}) custom-call(bf16[2,4096,512]{2,1,0:T(8,128)(2,1)} %basis_ref.1), custom_call_target="tpu_custom_call" | custom-call | flops 10000000000 | bytes 16777216 | tf_op jit(solution)/shard_map/pallas_call | solution.py:52
  22.6 1.2 %slice.11 = bf16[1,1]{1,0:T(2,128)(2,1)} slice(bf16[16,128]{1,0:T(8,128)(2,1)} %get-tuple-element.13), slice={[0:1], [0:1]} | slice | bytes 4 | tf_op jit(solution)/shard_map/slice | solution.py:481
  24.1 0.8 maximum_add_fusion.side_ref
  24.9 1.3 %collective-permute-start.4 = (bf16[512,1024]{1,0:T(8,128)(2,1)S(1)}, bf16[512,1024]{1,0:T(8,128)(2,1)}, u32[]{:S(2)}, u32[]{:S(2)}) collective-permute-start(bf16[512,1024]{1,0:T(8,128)(2,1)S(1)} %maximum_add_fusion.side_ref), channel_id=1, source_target_pairs={{0,1},{1,0},{2,3},{3,2},{4,5},{5,4},{6,7},{7,6},{8,9},{9,8},{10,11... | collective-permute-start | bytes 3145736 | tf_op jit(solution)/shard_map/ppermute | solution.py:465
  26.9 2.7 %collective-permute-done.1.sib_ref = bf16[256,1536]{1,0:T(8,128)(2,1)S(1)} collective-permute-done((bf16[256,1536]{1,0:T(8,128)(2,1)S(1)}, bf16[256,1536]{1,0:T(8,128)(2,1)S(1)}, u32[]{:S(2)}, u32[]{:S(2)}) %collective-permute-start.1) | collective-permute-done | bytes 786464 | tf_op jit(solution)/shard_map/ppermute | solution.py:465
  29.6 11.3 %shard_map.119 = (bf16[2,256,4096]{2,1,0:T(8,128)(2,1)}, f32[72,128]{1,0:T(8,128)S(1)}) custom-call(s32[12]{0:T(128)S(1)} %concatenate.6.scal_ref, bf16[256,1536]{1,0:T(8,128)(2,1)S(1)} %copy-done.1, bf16[256,1536]{1,0:T(8,128)(2,1)S(1)} %collective-permute-done.1.sib_ref, bf16[512,1024]{1,0:T(8,128)(2,1)} %copy-done.6, ...), custom_call_target="tpu_custom_call" | custom-call | tf_op jit(solution)/shard_map/pallas_call | solution.py:193
  41.7 0.6 collective-permute-done.5
  42.3 7.2 %collective-permute-start.7 = (f32[72,128]{1,0:T(8,128)S(1)}, f32[72,128]{1,0:T(8,128)S(1)}, u32[]{:S(2)}, u32[]{:S(2)}) collective-permute-start(f32[72,128]{1,0:T(8,128)S(1)} %add.22.x_ref), channel_id=1, source_target_pairs={{0,254},{2,4},{4,2},{6,8},{8,6},{10,12},{12,10},{14,16},{16,14},{1... | collective-permute-start | bytes 110600 | tf_op jit(solution)/shard_map/ppermute | solution.py:462
  49.5 0.9 collective-permute-start.9
  50.4 6.7 %shard_map.120.hid_hbm = f32[2,256,4096]{2,1,0:T(8,128)} custom-call(bf16[256,256]{1,0:T(8,128)(2,1)S(1)} %copy-done.5, bf16[2,256,4096]{2,1,0:T(8,128)(2,1)} %get-tuple-element.16.hid_ref), custom_call_target="tpu_custom_call" | custom-call | flops 10000000000 | bytes 12582912 | tf_op jit(solution)/shard_map/pallas_call | solution.py:225
  57.1 0.9 collective-permute-done.9.odd2_ref
  58.0 11.3 %shard_map.121 = (f32[2,512,512]{2,1,0:T(8,128)}, bf16[2,512,512]{2,1,0:T(8,128)(2,1)S(1)}) custom-call(s32[12]{0:T(128)S(1)} %concatenate.6.scal_ref, f32[72,128]{1,0:T(8,128)S(1)} %add.22.x_ref, f32[72,128]{1,0:T(8,128)S(1)} %collective-permute-done.6.even_ref, f32[72,128]{1,0:T(8,128)S(1)} %collective-permute-done.7.odd_ref, ...), custom_call_target="tpu_custom_call" | custom-call | tf_op jit(solution)/shard_map/pallas_call | solution.py:328
  69.4 1.9 %collective-permute-start.10 = (bf16[2,512,512]{2,1,0:T(8,128)(2,1)S(1)}, bf16[2,512,512]{2,1,0:T(8,128)(2,1)S(1)}, u32[]{:S(2)}, u32[]{:S(2)}) collective-permute-start(bf16[2,512,512]{2,1,0:T(8,128)(2,1)S(1)} %get-tuple-element.18), channel_id=1, source_target_pairs={{0,1},{1,0},{2,3},{3,2},{4,5},{5,4},{6,7},{7,6},{8,9},{9,8},{10,11... | collective-permute-start | bytes 3145736 | tf_op jit(solution)/shard_map/ppermute | solution.py:465
  71.3 2.2 %collective-permute-done.other_ref = s32[12]{0:T(128)S(1)} collective-permute-done((s32[12]{0:T(128)S(1)}, s32[12]{0:T(128)S(1)}, u32[]{:S(2)}, u32[]{:S(2)}) %collective-permute-start) | collective-permute-done | bytes 80 | tf_op jit(solution)/shard_map/ppermute | solution.py:465
  73.5 1.6 %copy-done = f32[2,512,512]{2,1,0:T(8,128)S(1)} copy-done((f32[2,512,512]{2,1,0:T(8,128)S(1)}, f32[2,512,512]{2,1,0:T(8,128)}, u32[]{:S(2)}) %copy-start) | copy-done | bytes 2097176
  75.1 1.6 %shard_map.123 = (bf16[256,1024]{1,0:T(8,128)(2,1)S(1)}, bf16[256,1024]{1,0:T(8,128)(2,1)S(1)}) custom-call(s32[12]{0:T(128)S(1)} %concatenate.6.scal_ref, s32[12]{0:T(128)S(1)} %collective-permute-done.other_ref, f32[2,512,512]{2,1,0:T(8,128)S(1)} %copy-done, bf16[2,512,512]{2,1,0:T(8,128)(2,1)S(1)} %collective-permute-done.10.got_ref), custom_call_target="tpu_custom_call" | custom-call | tf_op jit(solution)/shard_map/pallas_call | solution.py:386
  76.7 1.7 %collective-permute-start.11 = (bf16[256,1024]{1,0:T(8,128)(2,1)S(1)}, bf16[256,1024]{1,0:T(8,128)(2,1)S(1)}, u32[]{:S(2)}, u32[]{:S(2)}) collective-permute-start(bf16[256,1024]{1,0:T(8,128)(2,1)S(1)} %get-tuple-element.19), channel_id=1, source_target_pairs={{0,2},{2,4},{4,6},{6,8},{8,10},{10,12},{12,14},{14,16},{16,18},{18... | collective-permute-start | bytes 1572872 | tf_op jit(solution)/shard_map/ppermute | solution.py:458
  78.4 5.2 %collective-permute-start.12 = (bf16[256,1024]{1,0:T(8,128)(2,1)S(1)}, bf16[256,1024]{1,0:T(8,128)(2,1)S(1)}, u32[]{:S(2)}, u32[]{:S(2)}) collective-permute-start(bf16[256,1024]{1,0:T(8,128)(2,1)S(1)} %get-tuple-element.20), channel_id=1, source_target_pairs={{0,254},{2,0},{4,2},{6,4},{8,6},{10,8},{12,10},{14,12},{16,14},{18... | collective-permute-start | bytes 1572872 | tf_op jit(solution)/shard_map/ppermute | solution.py:458
  83.7 1.3 %shard_map.122.own_ref = f32[256,1536]{1,0:T(8,128)S(1)} custom-call(s32[12]{0:T(128)S(1)} %concatenate.6.scal_ref, s32[12]{0:T(128)S(1)} %collective-permute-done.other_ref, f32[2,512,512]{2,1,0:T(8,128)S(1)} %copy-done, bf16[2,512,512]{2,1,0:T(8,128)(2,1)S(1)} %collective-permute-done.10.got_ref), custom_call_target="tpu_custom_call" | custom-call | flops 1000000000 | bytes 4194304 | tf_op jit(solution)/shard_map/pallas_call | solution.py:401
  85.0 10.4 %collective-permute-done.11.left_ref = bf16[256,1024]{1,0:T(8,128)(2,1)S(1)} collective-permute-done((bf16[256,1024]{1,0:T(8,128)(2,1)S(1)}, bf16[256,1024]{1,0:T(8,128)(2,1)S(1)}, u32[]{:S(2)}, u32[]{:S(2)}) %collective-permute-start.11) | collective-permute-done | bytes 524320 | tf_op jit(solution)/shard_map/ppermute | solution.py:458
  95.3 1.2 %shard_map.124 = f32[256,1536]{1,0:T(8,128)} custom-call(f32[256,1536]{1,0:T(8,128)S(1)} %shard_map.122.own_ref, bf16[256,1024]{1,0:T(8,128)(2,1)S(1)} %collective-permute-done.11.left_ref, bf16[256,1024]{1,0:T(8,128)(2,1)S(1)} %collective-permute-done.12.right_ref), custom_call_target="tpu_custom_call" | custom-call | tf_op jit(solution)/shard_map/pallas_call | solution.py:429
  (50 shorter events, 1.8 us)
Async XLA Ops:
  1.3 22.8 %collective-permute-start.2 = (bf16[256,1024]{1,0:T(8,128)(2,1)S(1)}, bf16[256,1024]{1,0:T(8,128)(2,1)S(1)}, u32[]{:S(2)}, u32[]{:S(2)}) collective-permute-start(bf16[256,1024]{1,0:T(8,128)(2,1)S(1)} %get-tuple-element.21), channel_id=1, source_target_pairs={{0,2},{2,4},{4,6},{6,8},{8,10},{10,12},{12,14},{14,16},{16,18},{18... | collective-permute-start | bytes 1572872 | tf_op jit(solution)/shard_map/ppermute | solution.py:458
  3.5 20.6 %collective-permute-start.3 = (bf16[256,1024]{1,0:T(8,128)(2,1)S(1)}, bf16[256,1024]{1,0:T(8,128)(2,1)S(1)}, u32[]{:S(2)}, u32[]{:S(2)}) collective-permute-start(bf16[256,1024]{1,0:T(8,128)(2,1)S(1)} %get-tuple-element.22), channel_id=1, source_target_pairs={{0,254},{2,0},{4,2},{6,4},{8,6},{10,8},{12,10},{14,12},{16,14},{18... | collective-permute-start | bytes 1572872 | tf_op jit(solution)/shard_map/ppermute | solution.py:458
  22.6 3.7 %copy-start.9 = (s32[2,4]{1,0:T(2,128)S(1)}, s32[2,4]{1,0:T(2,128)}, u32[]{:S(2)}) copy-start(s32[2,4]{1,0:T(2,128)} %param.14) | copy-start | bytes 100
  22.6 3.8 %copy-start.10 = (f32[256]{0:T(256)S(1)}, f32[256]{0:T(256)}, u32[]{:S(2)}) copy-start(f32[256]{0:T(256)} %param.17) | copy-start | bytes 3076
  22.6 3.9 %copy-start.11 = (f32[256]{0:T(256)S(1)}, f32[256]{0:T(256)}, u32[]{:S(2)}) copy-start(f32[256]{0:T(256)} %param.18) | copy-start | bytes 3076
  22.6 4.1 %copy-start.7 = (bf16[256,64]{0,1:T(8,128)(2,1)S(1)}, bf16[256,64]{0,1:T(8,128)(2,1)}, u32[]{:S(2)}) copy-start(bf16[256,64]{0,1:T(8,128)(2,1)} %param.19) | copy-start | bytes 98308
  22.6 7.0 %copy-start.2 = (f32[2,4096]{1,0:T(2,128)S(1)}, f32[2,4096]{1,0:T(2,128)}, u32[]{:S(2)}) copy-start(f32[2,4096]{1,0:T(2,128)} %w_ref.3) | copy-start | bytes 98308
  22.6 7.0 %copy-start.3 = (s32[2,4096]{1,0:T(2,128)S(1)}, s32[2,4096]{1,0:T(2,128)}, u32[]{:S(2)}) copy-start(s32[2,4096]{1,0:T(2,128)} %atom_ref.3) | copy-start | bytes 98308
  24.8 4.7 %copy-start.6 = (bf16[512,1024]{1,0:T(8,128)(2,1)}, bf16[512,1024]{1,0:T(8,128)(2,1)S(1)}, u32[]{:S(2)}) copy-start(bf16[512,1024]{1,0:T(8,128)(2,1)S(1)} %maximum_add_fusion.side_ref) | copy-start | bytes 3145732
  24.9 4.7 %collective-permute-start.4 = (bf16[512,1024]{1,0:T(8,128)(2,1)S(1)}, bf16[512,1024]{1,0:T(8,128)(2,1)}, u32[]{:S(2)}, u32[]{:S(2)}) collective-permute-start(bf16[512,1024]{1,0:T(8,128)(2,1)S(1)} %maximum_add_fusion.side_ref), channel_id=1, source_target_pairs={{0,1},{1,0},{2,3},{3,2},{4,5},{5,4},{6,7},{7,6},{8,9},{9,8},{10,11... | collective-permute-start | bytes 3145736 | tf_op jit(solution)/shard_map/ppermute | solution.py:465
  26.2 3.4 %collective-permute-start.1 = (bf16[256,1536]{1,0:T(8,128)(2,1)S(1)}, bf16[256,1536]{1,0:T(8,128)(2,1)S(1)}, u32[]{:S(2)}, u32[]{:S(2)}) collective-permute-start(bf16[256,1536]{1,0:T(8,128)(2,1)S(1)} %copy-done.1), channel_id=1, source_target_pairs={{0,1},{1,0},{2,3},{3,2},{4,5},{5,4},{6,7},{7,6},{8,9},{9,8},{10,11... | collective-permute-start | bytes 2359304 | tf_op jit(solution)/shard_map/ppermute | solution.py:465
  29.6 11.8 %copy-start.12 = (bf16[256]{0:T(256)(128)(2,1)S(1)}, bf16[256]{0:T(256)(128)(2,1)}, u32[]{:S(2)}) copy-start(bf16[256]{0:T(256)(128)(2,1)} %param.23) | copy-start | bytes 1540
  29.6 11.9 %copy-start.8 = (f32[256]{0:T(256)S(1)}, f32[256]{0:T(256)}, u32[]{:S(2)}) copy-start(f32[256]{0:T(256)} %param.22) | copy-start | bytes 3076
  29.6 20.8 %copy-start.5 = (bf16[256,256]{1,0:T(8,128)(2,1)S(1)}, bf16[256,256]{1,0:T(8,128)(2,1)}, u32[]{:S(2)}) copy-start(bf16[256,256]{1,0:T(8,128)(2,1)} %hw_ref.1) | copy-start | bytes 393220
  40.9 1.3 %collective-permute-start.5 = (f32[72,128]{1,0:T(8,128)S(1)}, f32[72,128]{1,0:T(8,128)S(1)}, u32[]{:S(2)}, u32[]{:S(2)}) collective-permute-start(f32[72,128]{1,0:T(8,128)S(1)} %get-tuple-element.15), channel_id=1, source_target_pairs={{0,1},{1,0},{2,3},{3,2},{4,5},{5,4},{6,7},{7,6},{8,9},{9,8},{10,11... | collective-permute-start | bytes 110600 | tf_op jit(solution)/shard_map/ppermute | solution.py:465
  42.3 14.9 %collective-permute-start.6 = (f32[72,128]{1,0:T(8,128)S(1)}, f32[72,128]{1,0:T(8,128)S(1)}, u32[]{:S(2)}, u32[]{:S(2)}) collective-permute-start(f32[72,128]{1,0:T(8,128)S(1)} %add.22.x_ref), channel_id=1, source_target_pairs={{0,2},{2,0},{4,6},{6,4},{8,10},{10,8},{12,14},{14,12},{16,18},{18,... | collective-permute-start | bytes 110600 | tf_op jit(solution)/shard_map/ppermute | solution.py:462
  42.3 14.9 %collective-permute-start.7 = (f32[72,128]{1,0:T(8,128)S(1)}, f32[72,128]{1,0:T(8,128)S(1)}, u32[]{:S(2)}, u32[]{:S(2)}) collective-permute-start(f32[72,128]{1,0:T(8,128)S(1)} %add.22.x_ref), channel_id=1, source_target_pairs={{0,254},{2,4},{4,2},{6,8},{8,6},{10,12},{12,10},{14,16},{16,14},{1... | collective-permute-start | bytes 110600 | tf_op jit(solution)/shard_map/ppermute | solution.py:462
  49.5 7.6 %collective-permute-start.8 = (f32[72,128]{1,0:T(8,128)S(1)}, f32[72,128]{1,0:T(8,128)S(1)}, u32[]{:S(2)}, u32[]{:S(2)}) collective-permute-start(f32[72,128]{1,0:T(8,128)S(1)} %add.22.x_ref), channel_id=1, source_target_pairs={{0,4},{2,6},{4,0},{6,2},{8,12},{10,14},{12,8},{14,10},{16,20},{18,... | collective-permute-start | bytes 110600 | tf_op jit(solution)/shard_map/ppermute | solution.py:462
  49.5 8.5 %collective-permute-start.9 = (f32[72,128]{1,0:T(8,128)S(1)}, f32[72,128]{1,0:T(8,128)S(1)}, u32[]{:S(2)}, u32[]{:S(2)}) collective-permute-start(f32[72,128]{1,0:T(8,128)S(1)} %add.22.x_ref), channel_id=1, source_target_pairs={{0,252},{2,254},{4,8},{6,10},{8,4},{10,6},{12,16},{14,18},{16,12},... | collective-permute-start | bytes 110600 | tf_op jit(solution)/shard_map/ppermute | solution.py:462
  50.4 7.6 %copy-start.4 = (bf16[64,256]{1,0:T(8,128)(2,1)S(1)}, bf16[64,256]{1,0:T(8,128)(2,1)}, u32[]{:S(2)}) copy-start(bf16[64,256]{1,0:T(8,128)(2,1)} %atom_in_ref.1) | copy-start | bytes 98308
  69.4 4.2 %collective-permute-start.10 = (bf16[2,512,512]{2,1,0:T(8,128)(2,1)S(1)}, bf16[2,512,512]{2,1,0:T(8,128)(2,1)S(1)}, u32[]{:S(2)}, u32[]{:S(2)}) collective-permute-start(bf16[2,512,512]{2,1,0:T(8,128)(2,1)S(1)} %get-tuple-element.18), channel_id=1, source_target_pairs={{0,1},{1,0},{2,3},{3,2},{4,5},{5,4},{6,7},{7,6},{8,9},{9,8},{10,11... | collective-permute-start | bytes 3145736 | tf_op jit(solution)/shard_map/ppermute | solution.py:465
  71.2 2.3 %collective-permute-start = (s32[12]{0:T(128)S(1)}, s32[12]{0:T(128)S(1)}, u32[]{:S(2)}, u32[]{:S(2)}) collective-permute-start(s32[12]{0:T(128)S(1)} %concatenate.6.scal_ref), channel_id=1, source_target_pairs={{0,1},{1,0},{2,3},{3,2},{4,5},{5,4},{6,7},{7,6},{8,9},{9,8},{10,11... | collective-permute-start | bytes 152 | tf_op jit(solution)/shard_map/ppermute | solution.py:465
  76.7 18.6 %collective-permute-start.11 = (bf16[256,1024]{1,0:T(8,128)(2,1)S(1)}, bf16[256,1024]{1,0:T(8,128)(2,1)S(1)}, u32[]{:S(2)}, u32[]{:S(2)}) collective-permute-start(bf16[256,1024]{1,0:T(8,128)(2,1)S(1)} %get-tuple-element.19), channel_id=1, source_target_pairs={{0,2},{2,4},{4,6},{6,8},{8,10},{10,12},{12,14},{14,16},{16,18},{18... | collective-permute-start | bytes 1572872 | tf_op jit(solution)/shard_map/ppermute | solution.py:458
  78.4 16.9 %collective-permute-start.12 = (bf16[256,1024]{1,0:T(8,128)(2,1)S(1)}, bf16[256,1024]{1,0:T(8,128)(2,1)S(1)}, u32[]{:S(2)}, u32[]{:S(2)}) collective-permute-start(bf16[256,1024]{1,0:T(8,128)(2,1)S(1)} %get-tuple-element.20), channel_id=1, source_target_pairs={{0,254},{2,0},{4,2},{6,4},{8,6},{10,8},{12,10},{14,12},{16,14},{18... | collective-permute-start | bytes 1572872 | tf_op jit(solution)/shard_map/ppermute | solution.py:458
  (2 other events, 5.2 us)

commit v2 on v1

--- a/solution.py
+++ b/solution.py
@@ -17,6 +17,7 @@
 CHIPA = 32
 SEGS = 96
 TILE = 2048
+FIRST = (1024, 1024)
 TRANS = 1024
 MIB = 2**20
 XROWS = 72
@@ -55,11 +56,11 @@
         in_specs=[pl.BlockSpec((1, TRANS, funcs), lambda b, t: (b, t, 0))],
         out_specs=[
             pl.BlockSpec((1, funcs, TRANS), lambda b, t: (b, 0, t)),
-            pl.BlockSpec((16, 128), lambda b, t: (0, 0)),
+            pl.BlockSpec((1, 2 * CHIPF), lambda b, t: (0, 0)),
         ],
         out_shape=[
             jax.ShapeDtypeStruct((batches, funcs, points), bf16),
-            jax.ShapeDtypeStruct((16, 128), bf16),
+            jax.ShapeDtypeStruct((1, 2 * CHIPF), bf16),
         ],
         compiler_params=pltpu.CompilerParams(vmem_limit_bytes=56 * MIB),
         cost_estimate=pl.CostEstimate(
@@ -69,8 +70,11 @@
 
 
 def tiles_of(points, batches):
-    per = points // TILE
-    return [(b, pl.ds(t * TILE, TILE)) for b in range(batches) for t in range(per)]
+    sizes = [[TILE] * (points // TILE) for _ in range(batches)]
+    sizes[0] = list(FIRST) + sizes[0][1:]
+    return [
+        (b, pl.ds(sum(row[:i]), row[i])) for b, row in enumerate(sizes) for i in range(len(row))
+    ]
 
 
 def fetch(src, dst, tiles, sems):
@@ -156,8 +160,8 @@
         atom = atom_ref[b : b + 1, cols] - atom_start
         w_high = w.astype(bf16).astype(f32)
         w_low = w - w_high
-        match = lax.broadcasted_iota(jnp.int32, (SEGS, TILE), 0) == atom
-        zero = jnp.zeros((SEGS, TILE), f32)
+        match = lax.broadcasted_iota(jnp.int32, (SEGS, cols.size), 0) == atom
+        zero = jnp.zeros((SEGS, cols.size), f32)
         member = jnp.concatenate(
             [jnp.where(match, w_high, zero), jnp.where(match, w_low, zero)], axis=0
         ).astype(bf16)
@@ -166,7 +170,7 @@
         )
         part = jnp.where(match, w * w, zero)
         total = part[:, :128]
-        for j in range(1, TILE // 128):
+        for j in range(1, cols.size // 128):
             total = total + part[:, j * 128 : (j + 1) * 128]
         squares[...] += total
 
@@ -189,7 +193,7 @@
 
 def first_pass(scal, rows, bt, w, atom, in_w, in_b, proj):
     batches, funcs, points = bt.shape
-    tiles = batches * points // TILE
+    tiles = len(tiles_of(points, batches))
     return pl.pallas_call(
         first_kernel,
         in_specs=[SMEM] + [VMEM] * 4 + [ANY] + [VMEM] * 5,
@@ -211,49 +215,26 @@
     )(scal, *rows, bt, w, atom, in_w, in_b, proj)
 
 
-def layer_kernel(hw_ref, hid_ref, out_ref, hw_t):
-    @pl.when((pl.program_id(0) == 0) & (pl.program_id(1) == 0))
-    def _():
-        hw_t[...] = (0.5 * hw_ref[...].astype(f32)).T.astype(bf16)
-
-    out_ref[0] = jnp.dot(hw_t[...], hid_ref[0], preferred_element_type=f32)
-
-
-def layer(hw, hid):
-    batches, units, points = hid.shape
-    spec = pl.BlockSpec((1, units, TILE), lambda b, t: (b, 0, t))
-    return pl.pallas_call(
-        layer_kernel,
-        grid=(batches, points // TILE),
-        in_specs=[pl.BlockSpec((units, units), lambda b, t: (0, 0)), spec],
-        out_specs=spec,
-        out_shape=jax.ShapeDtypeStruct(hid.shape, f32),
-        scratch_shapes=[pltpu.VMEM((units, units), bf16)],
-        compiler_params=pltpu.CompilerParams(vmem_limit_bytes=52 * MIB),
-        cost_estimate=pl.CostEstimate(
-            flops=10**10, bytes_accessed=6 * hid.size, transcendentals=0
-        ),
-    )(hw, hid)
-
-
 def second_kernel(
     scal_ref,
     x_ref,
-    even_ref,
-    odd_ref,
-    even2_ref,
-    odd2_ref,
+    l1_ref,
+    l2_ref,
+    r1_ref,
+    r2_ref,
     atom_in_ref,
+    hw_ref,
     hb_ref,
     ow_ref,
     w_ref,
     atom_ref,
     hid_hbm,
     bt_hbm,
+    out_ref,
     mats_ref,
-    send_ref,
     hid_ref,
     bt_ref,
+    hw_t,
     feature,
     hid_sems,
     bt_sems,
@@ -266,22 +247,15 @@
         hid_load.start()
         bt_load.start()
 
-    first = scal_ref[10] == 0
-    first2 = scal_ref[11] == 0
-    left1 = jnp.where(first, odd_ref[...], even_ref[...])
-    right1 = jnp.where(first, even_ref[...], odd_ref[...])
-    left2 = jnp.where(first2, odd2_ref[...], even2_ref[...])
-    right2 = jnp.where(first2, even2_ref[...], odd2_ref[...])
-
     def part(x, start, size):
         return x[:, start * CHIPA : (start + size) * CHIPA]
 
     zero = jnp.zeros((XROWS, 2 * CHIPA), f32)
     total = x_ref[:, :SEGS]
-    total = total + jnp.concatenate([part(left1, 1, 2), zero[:, :CHIPA]], axis=1)
-    total = total + jnp.concatenate([part(left2, 2, 1), zero], axis=1)
-    total = total + jnp.concatenate([zero[:, :CHIPA], part(right1, 0, 2)], axis=1)
-    total = total + jnp.concatenate([zero, part(right2, 0, 1)], axis=1)
+    total = total + jnp.concatenate([part(l1_ref, 1, 2), zero[:, :CHIPA]], axis=1)
+    total = total + jnp.concatenate([part(l2_ref, 2, 1), zero], axis=1)
+    total = total + jnp.concatenate([zero[:, :CHIPA], part(r1_ref, 0, 2)], axis=1)
+    total = total + jnp.concatenate([zero, part(r2_ref, 0, 1)], axis=1)
     scaled = total[:ATW] / jnp.sqrt(total[ATW : ATW + 1] + eps_atom)
     value = jnp.dot(
         atom_in_ref[...].T, scaled.astype(bf16), preferred_element_type=f32
@@ -290,18 +264,19 @@
     high = value.astype(bf16)
     low = (value - high.astype(f32)).astype(bf16)
     feature[...] = jnp.concatenate([high, low], axis=1)
+    hw_t[...] = (0.5 * hw_ref[...].astype(f32)).T.astype(bf16)
     mats_ref[...] = jnp.zeros_like(mats_ref)
 
     def weigh(i):
         b, cols = tiles[i]
         atom = atom_ref[b : b + 1, cols] - atom_start
-        ids = lax.broadcasted_iota(jnp.int32, (SEGS, TILE), 0)
+        ids = lax.broadcasted_iota(jnp.int32, (SEGS, cols.size), 0)
         match = (ids == atom).astype(f32)
         member = jnp.concatenate([match, match], axis=0).astype(bf16)
         hid_loads[i].wait()
-        half = hid_ref[b, :, cols] + jnp.dot(
-            feature[...], member, preferred_element_type=f32
-        )
+        half = jnp.dot(
+            hw_t[...], hid_ref[b, :, cols], preferred_element_type=f32
+        ) + jnp.dot(feature[...], member, preferred_element_type=f32)
         second = silu_of_twice(half)
         point = jnp.sum(second * ow_ref[...], axis=0, keepdims=True)
         scale = w_ref[b : b + 1, cols] * point
@@ -319,29 +294,28 @@
 
     for i in range(len(tiles)):
         gram(i, weigh(i))
-    send_ref[...] = mats_ref[...].astype(bf16)
-
-
-def second_pass(scal, sums, atom_in, hb, ow, w, atom, hid, bt):
+    out_ref[...] = mats_ref[...].astype(bf16)
+
+
+def second_pass(scal, sums, atom_in, hw, hb, ow, w, atom, hid, bt):
     batches, funcs, points = bt.shape
-    tiles = batches * points // TILE
+    tiles = len(tiles_of(points, batches))
     return pl.pallas_call(
         second_kernel,
-        in_specs=[SMEM] + [VMEM] * 10 + [ANY] * 2,
-        out_specs=[VMEM] * 2,
-        out_shape=[
-            jax.ShapeDtypeStruct((batches, SIGF, SIGF), f32),
-            jax.ShapeDtypeStruct((batches, SIGF, SIGF), bf16),
-        ],
+        in_specs=[SMEM] + [VMEM] * 11 + [ANY] * 2,
+        out_specs=VMEM,
+        out_shape=jax.ShapeDtypeStruct((batches, SIGF, SIGF), bf16),
         scratch_shapes=[
-            pltpu.VMEM(hid.shape, f32),
+            pltpu.VMEM((batches, SIGF, SIGF), f32),
+            pltpu.VMEM(hid.shape, bf16),
             pltpu.VMEM(bt.shape, bf16),
+            pltpu.VMEM((HID, HID), bf16),
             pltpu.VMEM((HID, 2 * SEGS), bf16),
             pltpu.SemaphoreType.DMA((tiles,)),
             pltpu.SemaphoreType.DMA((tiles,)),
         ],
         compiler_params=pltpu.CompilerParams(vmem_limit_bytes=52 * MIB),
-    )(scal, *sums, atom_in, hb, ow, w, atom, hid, bt)
+    )(scal, *sums, atom_in, hw, hb, ow, w, atom, hid, bt)
 
 
 def scatter(scal_ref, other_ref, mats_ref, got_ref, targets):
@@ -457,10 +431,6 @@
     def shift(x, by):
         return lax.ppermute(x, "pts", [(i, (i + by) % chips) for i in range(chips)])
 
-    def pair(x, by, start):
-        to = lambda i: (((i - start) % chips) ^ by) + start
-        return lax.ppermute(x, "pts", [(i, to(i) % chips) for i in range(chips)])
-
     def swap(x):
         return lax.ppermute(x, "blk", [(0, 1), (1, 0)])
 
@@ -469,8 +439,6 @@
             (sig_blocks - CHIPB * (chip - 1)).reshape(-1),
             core[None].astype(jnp.int32),
             (CHIPA * (chip - 1))[None].astype(jnp.int32),
-            (chip % 2)[None].astype(jnp.int32),
-            ((chip // 2) % 2)[None].astype(jnp.int32),
         ]
     )
     from_left = shift(density[:, CHIPF:], 1)
@@ -478,7 +446,7 @@
     sibling = swap(density)
     other = swap(scal)
     bt, token = transpose_basis(basis_values)
-    side = jnp.concatenate([from_left, from_right], axis=0) + token[0, 0]
+    side = jnp.concatenate([from_left, from_right], axis=0) + token
     side_sib = swap(side)
 
     column = lambda x, by=1.0: (by * x.astype(f32)).reshape(HID, 1)
@@ -493,20 +461,20 @@
         atom_proj,
     )
     sums = sums + swap(sums)
-    near_sums = [pair(sums, by, start) for by, start in ((1, 0), (2, 0), (1, 1), (2, 2))]
-    half = layer(hidden_weight, hidden)
-    mats, send = second_pass(
+    near_sums = {by: shift(sums, by) for by in (1, 2, -1, -2)}
+    mats = second_pass(
         scal,
-        [sums, near_sums[0], near_sums[2], near_sums[1], near_sums[3]],
+        [sums] + [near_sums[by] for by in (1, 2, -1, -2)],
         atom_in,
+        hidden_weight,
         column(hidden_bias),
         column(out_weight),
         grid_weights,
         atom_of,
-        half,
+        hidden,
         bt,
     )
-    got = swap(send)
+    got = swap(mats)
     to_left, to_right = side_sums(scal, other, mats, got)
     own = own_sums(scal, other, mats, got)
     return final_sum(own, shift(to_right, 1), shift(to_left, -1))

time: 97 us -> 90.5 us (0.933)
  Pallas kernels: 43.4 us -> 36.5 us
  local copies, waits for them, and re-layouts: 5.01 us -> 2.11 us
  starting transfers between devices: 30.2 us -> 31.7 us
  waiting for transfers between devices: 16.9 us -> 18.3 us
    ppermute x4 -> x8, starting transfers between devices: 18.2 us -> 27.6 us  [shift(): return lax.ppermute(x, 'pts', [(i, (i + by) % chips) for i in range(chips)])]
    ppermute x4 -> x0, starting transfers between devices: 8.16 us -> none  [pair(): return lax.ppermute(x, 'pts', [(i, to(i) % chips) for i in range(chips)])]
    pallas_call x2 -> x1, Pallas kernels: 18 us -> 11 us  [second_pass(): pl.pallas_call(second_kernel, in_specs=[SMEM] + [VMEM] * 11 + [ANY] * 2,...]
    ppermute x4 -> x8, waiting for transfers between devices: 10.6 us -> 12.8 us  [shift(): return lax.ppermute(x, 'pts', [(i, (i + by) % chips) for i in range(chips)])]
    unnamed x27 -> x25, local copies, waits for them, and re-layouts: 1.77 us -> 0.18 us
    slice x1 -> x0, local copies, waits for them, and re-layouts: 1.23 us -> none  [on_device(): side = jnp.concatenate([from_left, from_right], axis=0) + token[0, 0]]
  transfers between devices with their start and end apart: 13 -> 13, of which waited for: 6 -> 6; matrix products, arithmetic and copies ran while one was open for 2% -> 2% of each run, Pallas kernels for 19% -> 13%
where the time goes in v2:
time: 90.5 us; the launch traced here: 90 us
  Pallas kernels  36.5 us (40%)
  starting transfers between devices  31.7 us (35%)
  waiting for transfers between devices  18.3 us (20%)
  local copies, waits for them, and re-layouts  2.11 us (2%)
  other arithmetic  1.1 us (1%)
    ppermute x8, starting transfers between devices, shift(): return lax.ppermute(x, 'pts', [(i, (i + by) % chips) for i in range(chips)])  27.6 us
    ppermute x8, waiting for transfers between devices, shift(): return lax.ppermute(x, 'pts', [(i, (i + by) % chips) for i in range(chips)])  12.8 us
    pallas_call x1, Pallas kernels, first_pass(): pl.pallas_call(first_kernel, in_specs=[SMEM] + [VMEM] * 4 + [ANY] + [VMEM...  11.4 us
    pallas_call x1, Pallas kernels, second_pass(): pl.pallas_call(second_kernel, in_specs=[SMEM] + [VMEM] * 11 + [ANY] * 2,...  11 us
    pallas_call x1, Pallas kernels, transpose_basis(): pl.pallas_call(transpose_kernel, grid=(batches, points // TRANS), in_spec...  10.1 us
    ppermute x5, waiting for transfers between devices, swap(): return lax.ppermute(x, 'blk', [(0, 1), (1, 0)])  5.53 us
    ppermute x5, starting transfers between devices, swap(): return lax.ppermute(x, 'blk', [(0, 1), (1, 0)])  4.13 us
  transfers between devices with their start and end apart: 13, of which 6 were waited for; matrix products, arithmetic and copies ran while one was open for 2% of the time, Pallas kernels for 13%

profile of v2, /device:TPU:1, one launch (start us, length us, event | category | flops | bytes accessed | tf_op | source)
XLA Modules:
  0.0 90.0 jit_solution(12006330380494007461)
XLA Ops:
  0.0 1.3 %fusion = (bf16[256,1024]{1,0:T(8,128)(2,1)S(1)}, bf16[256,1024]{1,0:T(8,128)(2,1)S(1)}) fusion(bf16[256,1536]{1,0:T(8,128)(2,1)} %own_ref.1), kind=kLoop, calls=%fused_computation.5 | loop fusion | bytes 2097152 | tf_op jit(solution)/shard_map/slice | solution.py:444
  1.3 2.2 %collective-permute-start.2 = (bf16[256,1024]{1,0:T(8,128)(2,1)S(1)}, bf16[256,1024]{1,0:T(8,128)(2,1)S(1)}, u32[]{:S(2)}, u32[]{:S(2)}) collective-permute-start(bf16[256,1024]{1,0:T(8,128)(2,1)S(1)} %get-tuple-element.17), channel_id=1, source_target_pairs={{0,2},{2,4},{4,6},{6,8},{8,10},{10,12},{12,14},{14,16},{16,18},{18... | collective-permute-start | bytes 1572872 | tf_op jit(solution)/shard_map/ppermute | solution.py:432
  3.5 9.0 %collective-permute-start.3 = (bf16[256,1024]{1,0:T(8,128)(2,1)S(1)}, bf16[256,1024]{1,0:T(8,128)(2,1)S(1)}, u32[]{:S(2)}, u32[]{:S(2)}) collective-permute-start(bf16[256,1024]{1,0:T(8,128)(2,1)S(1)} %get-tuple-element.18), channel_id=1, source_target_pairs={{0,254},{2,0},{4,2},{6,4},{8,6},{10,8},{12,10},{14,12},{16,14},{18... | collective-permute-start | bytes 1572872 | tf_op jit(solution)/shard_map/ppermute | solution.py:432
  12.5 10.1 %shard_map.118 = (bf16[2,512,4096]{2,1,0:T(8,128)(2,1)}, bf16[1,1024]{1,0:T(2,128)(2,1)}) custom-call(bf16[2,4096,512]{2,1,0:T(8,128)(2,1)} %basis_ref.1), custom_call_target="tpu_custom_call" | custom-call | flops 10000000000 | bytes 16777216 | tf_op jit(solution)/shard_map/pallas_call | solution.py:53
  22.7 0.8 reduce
  23.4 0.7 collective-permute-done.2
  24.1 0.2 maximum_add_fusion.side_ref
  24.3 1.3 %collective-permute-start.4 = (bf16[512,1024]{1,0:T(8,128)(2,1)S(1)}, bf16[512,1024]{1,0:T(8,128)(2,1)}, u32[]{:S(2)}, u32[]{:S(2)}) collective-permute-start(bf16[512,1024]{1,0:T(8,128)(2,1)S(1)} %maximum_add_fusion.side_ref), channel_id=1, source_target_pairs={{0,1},{1,0},{2,3},{3,2},{4,5},{5,4},{6,7},{7,6},{8,9},{9,8},{10,11... | collective-permute-start | bytes 3145736 | tf_op jit(solution)/shard_map/ppermute | solution.py:435
  26.4 2.7 %collective-permute-done.1.sib_ref = bf16[256,1536]{1,0:T(8,128)(2,1)S(1)} collective-permute-done((bf16[256,1536]{1,0:T(8,128)(2,1)S(1)}, bf16[256,1536]{1,0:T(8,128)(2,1)S(1)}, u32[]{:S(2)}, u32[]{:S(2)}) %collective-permute-start.1) | collective-permute-done | bytes 786464 | tf_op jit(solution)/shard_map/ppermute | solution.py:435
  29.1 11.4 %shard_map.119 = (bf16[2,256,4096]{2,1,0:T(8,128)(2,1)}, f32[72,128]{1,0:T(8,128)S(1)}) custom-call(s32[10]{0:T(128)S(1)} %pad_add_fusion.scal_ref, bf16[256,1536]{1,0:T(8,128)(2,1)S(1)} %copy-done, bf16[256,1536]{1,0:T(8,128)(2,1)S(1)} %collective-permute-done.1.sib_ref, bf16[512,1024]{1,0:T(8,128)(2,1)} %copy-done.5, ...), custom_call_target="tpu_custom_call" | custom-call | tf_op jit(solution)/shard_map/pallas_call | solution.py:197
  40.6 0.5 collective-permute-start.5
  41.1 0.9 collective-permute-done.5
  42.0 7.0 %collective-permute-start.8 = (f32[72,128]{1,0:T(8,128)S(1)}, f32[72,128]{1,0:T(8,128)S(1)}, u32[]{:S(2)}, u32[]{:S(2)}) collective-permute-start(f32[72,128]{1,0:T(8,128)S(1)} %add.17.x_ref), channel_id=1, source_target_pairs={{0,254},{2,0},{4,2},{6,4},{8,6},{10,8},{12,10},{14,12},{16,14},{18... | collective-permute-start | bytes 110600 | tf_op jit(solution)/shard_map/ppermute | solution.py:432
  49.1 2.3 %collective-permute-start.9 = (f32[72,128]{1,0:T(8,128)S(1)}, f32[72,128]{1,0:T(8,128)S(1)}, u32[]{:S(2)}, u32[]{:S(2)}) collective-permute-start(f32[72,128]{1,0:T(8,128)S(1)} %add.17.x_ref), channel_id=1, source_target_pairs={{0,252},{2,254},{4,0},{6,2},{8,4},{10,6},{12,8},{14,10},{16,12},{1... | collective-permute-start | bytes 110600 | tf_op jit(solution)/shard_map/ppermute | solution.py:432
  51.7 1.7 %collective-permute-done.9.r2_ref = f32[72,128]{1,0:T(8,128)S(1)} collective-permute-done((f32[72,128]{1,0:T(8,128)S(1)}, f32[72,128]{1,0:T(8,128)S(1)}, u32[]{:S(2)}, u32[]{:S(2)}) %collective-permute-start.9) | collective-permute-done | bytes 36896 | tf_op jit(solution)/shard_map/ppermute | solution.py:432
  53.4 11.0 %shard_map.120.mats_ref = bf16[2,512,512]{2,1,0:T(8,128)(2,1)S(1)} custom-call(s32[10]{0:T(128)S(1)} %pad_add_fusion.scal_ref, f32[72,128]{1,0:T(8,128)S(1)} %add.17.x_ref, f32[72,128]{1,0:T(8,128)S(1)} %collective-permute-done.6.l1_ref, f32[72,128]{1,0:T(8,128)S(1)} %collective-permute-done.7.l2_ref, f32[72,128]{1,0:T(8,128)S(1)} %collective-permute-done.8.r1_ref, ...), custom_call_target="tpu_custom_call" | custom-call | tf_op jit(solution)/shard_map/pallas_call | solution.py:303
  64.4 1.9 %collective-permute-start.10 = (bf16[2,512,512]{2,1,0:T(8,128)(2,1)S(1)}, bf16[2,512,512]{2,1,0:T(8,128)(2,1)S(1)}, u32[]{:S(2)}, u32[]{:S(2)}) collective-permute-start(bf16[2,512,512]{2,1,0:T(8,128)(2,1)S(1)} %shard_map.120.mats_ref), channel_id=1, source_target_pairs={{0,1},{1,0},{2,3},{3,2},{4,5},{5,4},{6,7},{7,6},{8,9},{9,8},{10,11... | collective-permute-start | bytes 3145736 | tf_op jit(solution)/shard_map/ppermute | solution.py:435
  66.3 0.3 collective-permute-start
  66.6 2.0 %collective-permute-done.other_ref = s32[10]{0:T(128)S(1)} collective-permute-done((s32[10]{0:T(128)S(1)}, s32[10]{0:T(128)S(1)}, u32[]{:S(2)}, u32[]{:S(2)}) %collective-permute-start) | collective-permute-done | bytes 72 | tf_op jit(solution)/shard_map/ppermute | solution.py:435
  68.6 1.6 %shard_map.122 = (bf16[256,1024]{1,0:T(8,128)(2,1)S(1)}, bf16[256,1024]{1,0:T(8,128)(2,1)S(1)}) custom-call(s32[10]{0:T(128)S(1)} %pad_add_fusion.scal_ref, s32[10]{0:T(128)S(1)} %collective-permute-done.other_ref, bf16[2,512,512]{2,1,0:T(8,128)(2,1)S(1)} %shard_map.120.mats_ref, bf16[2,512,512]{2,1,0:T(8,128)(2,1)S(1)} %collective-permute-done.10.got_ref), custom_call_target="tpu_custom_call" | custom-call | tf_op jit(solution)/shard_map/pallas_call | solution.py:360
  70.2 6.9 %collective-permute-start.12 = (bf16[256,1024]{1,0:T(8,128)(2,1)S(1)}, bf16[256,1024]{1,0:T(8,128)(2,1)S(1)}, u32[]{:S(2)}, u32[]{:S(2)}) collective-permute-start(bf16[256,1024]{1,0:T(8,128)(2,1)S(1)} %get-tuple-element.16), channel_id=1, source_target_pairs={{0,254},{2,0},{4,2},{6,4},{8,6},{10,8},{12,10},{14,12},{16,14},{18... | collective-permute-start | bytes 1572872 | tf_op jit(solution)/shard_map/ppermute | solution.py:432
  77.1 1.2 %shard_map.121.own_ref = f32[256,1536]{1,0:T(8,128)S(1)} custom-call(s32[10]{0:T(128)S(1)} %pad_add_fusion.scal_ref, s32[10]{0:T(128)S(1)} %collective-permute-done.other_ref, bf16[2,512,512]{2,1,0:T(8,128)(2,1)S(1)} %shard_map.120.mats_ref, bf16[2,512,512]{2,1,0:T(8,128)(2,1)S(1)} %collective-permute-done.10.got_ref), custom_call_target="tpu_custom_call" | custom-call | flops 1000000000 | bytes 4194304 | tf_op jit(solution)/shard_map/pallas_call | solution.py:375
  78.3 10.4 %collective-permute-done.11.left_ref = bf16[256,1024]{1,0:T(8,128)(2,1)S(1)} collective-permute-done((bf16[256,1024]{1,0:T(8,128)(2,1)S(1)}, bf16[256,1024]{1,0:T(8,128)(2,1)S(1)}, u32[]{:S(2)}, u32[]{:S(2)}) %collective-permute-start.11) | collective-permute-done | bytes 524320 | tf_op jit(solution)/shard_map/ppermute | solution.py:432
  88.8 1.2 %shard_map.123 = f32[256,1536]{1,0:T(8,128)} custom-call(f32[256,1536]{1,0:T(8,128)S(1)} %shard_map.121.own_ref, bf16[256,1024]{1,0:T(8,128)(2,1)S(1)} %collective-permute-done.11.left_ref, bf16[256,1024]{1,0:T(8,128)(2,1)S(1)} %collective-permute-done.12.right_ref), custom_call_target="tpu_custom_call" | custom-call | tf_op jit(solution)/shard_map/pallas_call | solution.py:403
  (47 shorter events, 1.2 us)
Async XLA Ops:
  1.3 22.8 %collective-permute-start.2 = (bf16[256,1024]{1,0:T(8,128)(2,1)S(1)}, bf16[256,1024]{1,0:T(8,128)(2,1)S(1)}, u32[]{:S(2)}, u32[]{:S(2)}) collective-permute-start(bf16[256,1024]{1,0:T(8,128)(2,1)S(1)} %get-tuple-element.17), channel_id=1, source_target_pairs={{0,2},{2,4},{4,6},{6,8},{8,10},{10,12},{12,14},{14,16},{16,18},{18... | collective-permute-start | bytes 1572872 | tf_op jit(solution)/shard_map/ppermute | solution.py:432
  3.5 20.6 %collective-permute-start.3 = (bf16[256,1024]{1,0:T(8,128)(2,1)S(1)}, bf16[256,1024]{1,0:T(8,128)(2,1)S(1)}, u32[]{:S(2)}, u32[]{:S(2)}) collective-permute-start(bf16[256,1024]{1,0:T(8,128)(2,1)S(1)} %get-tuple-element.18), channel_id=1, source_target_pairs={{0,254},{2,0},{4,2},{6,4},{8,6},{10,8},{12,10},{14,12},{16,14},{18... | collective-permute-start | bytes 1572872 | tf_op jit(solution)/shard_map/ppermute | solution.py:432
  22.6 3.2 %copy-start.8 = (s32[2,4]{1,0:T(2,128)S(1)}, s32[2,4]{1,0:T(2,128)}, u32[]{:S(2)}) copy-start(s32[2,4]{1,0:T(2,128)} %param.14) | copy-start | bytes 100
  22.6 3.3 %copy-start.9 = (f32[256]{0:T(256)S(1)}, f32[256]{0:T(256)}, u32[]{:S(2)}) copy-start(f32[256]{0:T(256)} %param.17) | copy-start | bytes 3076
  22.6 3.4 %copy-start.10 = (f32[256]{0:T(256)S(1)}, f32[256]{0:T(256)}, u32[]{:S(2)}) copy-start(f32[256]{0:T(256)} %param.18) | copy-start | bytes 3076
  22.6 3.5 %copy-start.6 = (bf16[256,64]{0,1:T(8,128)(2,1)S(1)}, bf16[256,64]{0,1:T(8,128)(2,1)}, u32[]{:S(2)}) copy-start(bf16[256,64]{0,1:T(8,128)(2,1)} %param.19) | copy-start | bytes 98308
  22.6 6.4 %copy-start.2 = (f32[2,4096]{1,0:T(2,128)S(1)}, f32[2,4096]{1,0:T(2,128)}, u32[]{:S(2)}) copy-start(f32[2,4096]{1,0:T(2,128)} %w_ref.3) | copy-start | bytes 98308
  22.6 6.4 %copy-start.3 = (s32[2,4096]{1,0:T(2,128)S(1)}, s32[2,4096]{1,0:T(2,128)}, u32[]{:S(2)}) copy-start(s32[2,4096]{1,0:T(2,128)} %atom_ref.3) | copy-start | bytes 98308
  24.3 4.7 %copy-start.5 = (bf16[512,1024]{1,0:T(8,128)(2,1)}, bf16[512,1024]{1,0:T(8,128)(2,1)S(1)}, u32[]{:S(2)}) copy-start(bf16[512,1024]{1,0:T(8,128)(2,1)S(1)} %maximum_add_fusion.side_ref) | copy-start | bytes 3145732
  24.3 4.7 %collective-permute-start.4 = (bf16[512,1024]{1,0:T(8,128)(2,1)S(1)}, bf16[512,1024]{1,0:T(8,128)(2,1)}, u32[]{:S(2)}, u32[]{:S(2)}) collective-permute-start(bf16[512,1024]{1,0:T(8,128)(2,1)S(1)} %maximum_add_fusion.side_ref), channel_id=1, source_target_pairs={{0,1},{1,0},{2,3},{3,2},{4,5},{5,4},{6,7},{7,6},{8,9},{9,8},{10,11... | collective-permute-start | bytes 3145736 | tf_op jit(solution)/shard_map/ppermute | solution.py:435
  25.7 3.4 %collective-permute-start.1 = (bf16[256,1536]{1,0:T(8,128)(2,1)S(1)}, bf16[256,1536]{1,0:T(8,128)(2,1)S(1)}, u32[]{:S(2)}, u32[]{:S(2)}) collective-permute-start(bf16[256,1536]{1,0:T(8,128)(2,1)S(1)} %copy-done), channel_id=1, source_target_pairs={{0,1},{1,0},{2,3},{3,2},{4,5},{5,4},{6,7},{7,6},{8,9},{9,8},{10,11... | collective-permute-start | bytes 2359304 | tf_op jit(solution)/shard_map/ppermute | solution.py:435
  29.1 22.3 %copy-start.11 = (bf16[256]{0:T(256)(128)(2,1)S(1)}, bf16[256]{0:T(256)(128)(2,1)}, u32[]{:S(2)}) copy-start(bf16[256]{0:T(256)(128)(2,1)} %param.23) | copy-start | bytes 1540
  29.1 22.4 %copy-start.7 = (f32[256]{0:T(256)S(1)}, f32[256]{0:T(256)}, u32[]{:S(2)}) copy-start(f32[256]{0:T(256)} %param.22) | copy-start | bytes 3076
  29.1 24.3 %copy-start.1 = (bf16[256,256]{1,0:T(8,128)(2,1)S(1)}, bf16[256,256]{1,0:T(8,128)(2,1)}, u32[]{:S(2)}) copy-start(bf16[256,256]{1,0:T(8,128)(2,1)} %hw_ref.1) | copy-start | bytes 393220
  29.1 24.3 %copy-start.4 = (bf16[64,256]{1,0:T(8,128)(2,1)S(1)}, bf16[64,256]{1,0:T(8,128)(2,1)}, u32[]{:S(2)}) copy-start(bf16[64,256]{1,0:T(8,128)(2,1)} %atom_in_ref.1) | copy-start | bytes 98308
  40.6 1.3 %collective-permute-start.5 = (f32[72,128]{1,0:T(8,128)S(1)}, f32[72,128]{1,0:T(8,128)S(1)}, u32[]{:S(2)}, u32[]{:S(2)}) collective-permute-start(f32[72,128]{1,0:T(8,128)S(1)} %get-tuple-element.13), channel_id=1, source_target_pairs={{0,1},{1,0},{2,3},{3,2},{4,5},{5,4},{6,7},{7,6},{8,9},{9,8},{10,11... | collective-permute-start | bytes 110600 | tf_op jit(solution)/shard_map/ppermute | solution.py:435
  41.9 9.7 %collective-permute-start.6 = (f32[72,128]{1,0:T(8,128)S(1)}, f32[72,128]{1,0:T(8,128)S(1)}, u32[]{:S(2)}, u32[]{:S(2)}) collective-permute-start(f32[72,128]{1,0:T(8,128)S(1)} %add.17.x_ref), channel_id=1, source_target_pairs={{0,2},{2,4},{4,6},{6,8},{8,10},{10,12},{12,14},{14,16},{16,18},{18... | collective-permute-start | bytes 110600 | tf_op jit(solution)/shard_map/ppermute | solution.py:432
  41.9 9.7 %collective-permute-start.7 = (f32[72,128]{1,0:T(8,128)S(1)}, f32[72,128]{1,0:T(8,128)S(1)}, u32[]{:S(2)}, u32[]{:S(2)}) collective-permute-start(f32[72,128]{1,0:T(8,128)S(1)} %add.17.x_ref), channel_id=1, source_target_pairs={{0,4},{2,6},{4,8},{6,10},{8,12},{10,14},{12,16},{14,18},{16,20},{1... | collective-permute-start | bytes 110600 | tf_op jit(solution)/shard_map/ppermute | solution.py:432
  42.0 9.6 %collective-permute-start.8 = (f32[72,128]{1,0:T(8,128)S(1)}, f32[72,128]{1,0:T(8,128)S(1)}, u32[]{:S(2)}, u32[]{:S(2)}) collective-permute-start(f32[72,128]{1,0:T(8,128)S(1)} %add.17.x_ref), channel_id=1, source_target_pairs={{0,254},{2,0},{4,2},{6,4},{8,6},{10,8},{12,10},{14,12},{16,14},{18... | collective-permute-start | bytes 110600 | tf_op jit(solution)/shard_map/ppermute | solution.py:432
  49.1 4.3 %collective-permute-start.9 = (f32[72,128]{1,0:T(8,128)S(1)}, f32[72,128]{1,0:T(8,128)S(1)}, u32[]{:S(2)}, u32[]{:S(2)}) collective-permute-start(f32[72,128]{1,0:T(8,128)S(1)} %add.17.x_ref), channel_id=1, source_target_pairs={{0,252},{2,254},{4,0},{6,2},{8,4},{10,6},{12,8},{14,10},{16,12},{1... | collective-permute-start | bytes 110600 | tf_op jit(solution)/shard_map/ppermute | solution.py:432
  64.4 4.2 %collective-permute-start.10 = (bf16[2,512,512]{2,1,0:T(8,128)(2,1)S(1)}, bf16[2,512,512]{2,1,0:T(8,128)(2,1)S(1)}, u32[]{:S(2)}, u32[]{:S(2)}) collective-permute-start(bf16[2,512,512]{2,1,0:T(8,128)(2,1)S(1)} %shard_map.120.mats_ref), channel_id=1, source_target_pairs={{0,1},{1,0},{2,3},{3,2},{4,5},{5,4},{6,7},{7,6},{8,9},{9,8},{10,11... | collective-permute-start | bytes 3145736 | tf_op jit(solution)/shard_map/ppermute | solution.py:435
  66.3 2.3 %collective-permute-start = (s32[10]{0:T(128)S(1)}, s32[10]{0:T(128)S(1)}, u32[]{:S(2)}, u32[]{:S(2)}) collective-permute-start(s32[10]{0:T(128)S(1)} %pad_add_fusion.scal_ref), channel_id=1, source_target_pairs={{0,1},{1,0},{2,3},{3,2},{4,5},{5,4},{6,7},{7,6},{8,9},{9,8},{10,11... | collective-permute-start | bytes 128 | tf_op jit(solution)/shard_map/ppermute | solution.py:435
  70.1 18.6 %collective-permute-start.11 = (bf16[256,1024]{1,0:T(8,128)(2,1)S(1)}, bf16[256,1024]{1,0:T(8,128)(2,1)S(1)}, u32[]{:S(2)}, u32[]{:S(2)}) collective-permute-start(bf16[256,1024]{1,0:T(8,128)(2,1)S(1)} %get-tuple-element.15), channel_id=1, source_target_pairs={{0,2},{2,4},{4,6},{6,8},{8,10},{10,12},{12,14},{14,16},{16,18},{18... | collective-permute-start | bytes 1572872 | tf_op jit(solution)/shard_map/ppermute | solution.py:432
  70.2 18.6 %collective-permute-start.12 = (bf16[256,1024]{1,0:T(8,128)(2,1)S(1)}, bf16[256,1024]{1,0:T(8,128)(2,1)S(1)}, u32[]{:S(2)}, u32[]{:S(2)}) collective-permute-start(bf16[256,1024]{1,0:T(8,128)(2,1)S(1)} %get-tuple-element.16), channel_id=1, source_target_pairs={{0,254},{2,0},{4,2},{6,4},{8,6},{10,8},{12,10},{14,12},{16,14},{18... | collective-permute-start | bytes 1572872 | tf_op jit(solution)/shard_map/ppermute | solution.py:432
  (1 other events, 3.1 us)

commit v3 on v2

--- a/solution.py
+++ b/solution.py
@@ -446,7 +446,7 @@
     sibling = swap(density)
     other = swap(scal)
     bt, token = transpose_basis(basis_values)
-    side = jnp.concatenate([from_left, from_right], axis=0) + token
+    side = jnp.concatenate([from_left, from_right], axis=0) + (token + 0 * sibling[:1, : 2 * CHIPF])
     side_sib = swap(side)
 
     column = lambda x, by=1.0: (by * x.astype(f32)).reshape(HID, 1)

time: 90.5 us -> 90.2 us (level)
    ppermute x8, starting transfers between devices: 27.6 us -> 25 us  [shift(): return lax.ppermute(x, 'pts', [(i, (i + by) % chips) for i in range(chips)])]
    ppermute x5, starting transfers between devices: 4.13 us -> 6.62 us  [swap(): return lax.ppermute(x, 'blk', [(0, 1), (1, 0)])]
  transfers between devices with their start and end apart: 13 -> 13, of which waited for: 6 -> 6; matrix products, arithmetic and copies ran while one was open for 2% -> 3% of each run, Pallas kernels for 13% -> 13%
where the time goes in v3:
time: 90.2 us; the launch traced here: 89.8 us
  Pallas kernels  36.6 us (41%)
  starting transfers between devices  31.6 us (35%)
  waiting for transfers between devices  18.1 us (20%)
  local copies, waits for them, and re-layouts  2.11 us (2%)
  other arithmetic  1.11 us (1%)
    ppermute x8, starting transfers between devices, shift(): return lax.ppermute(x, 'pts', [(i, (i + by) % chips) for i in range(chips)])  25 us
    ppermute x8, waiting for transfers between devices, shift(): return lax.ppermute(x, 'pts', [(i, (i + by) % chips) for i in range(chips)])  13.5 us
    pallas_call x1, Pallas kernels, first_pass(): pl.pallas_call(first_kernel, in_specs=[SMEM] + [VMEM] * 4 + [ANY] + [VMEM...  11.4 us
    pallas_call x1, Pallas kernels, second_pass(): pl.pallas_call(second_kernel, in_specs=[SMEM] + [VMEM] * 11 + [ANY] * 2,...  11 us
    pallas_call x1, Pallas kernels, transpose_basis(): pl.pallas_call(transpose_kernel, grid=(batches, points // TRANS), in_spec...  10.1 us
    ppermute x5, starting transfers between devices, swap(): return lax.ppermute(x, 'blk', [(0, 1), (1, 0)])  6.62 us
    ppermute x5, waiting for transfers between devices, swap(): return lax.ppermute(x, 'blk', [(0, 1), (1, 0)])  4.65 us
  transfers between devices with their start and end apart: 13, of which 6 were waited for; matrix products, arithmetic and copies ran while one was open for 3% of the time, Pallas kernels for 13%

profile of v3, /device:TPU:1, one launch (start us, length us, event | category | flops | bytes accessed | tf_op | source)
XLA Modules:
  0.0 89.8 jit_solution(6365171700161217586)
XLA Ops:
  0.0 3.2 %collective-permute-start.1 = (bf16[256,1536]{1,0:T(8,128)(2,1)}, bf16[256,1536]{1,0:T(8,128)(2,1)S(1)}, u32[]{:S(2)}, u32[]{:S(2)}) collective-permute-start(bf16[256,1536]{1,0:T(8,128)(2,1)} %own_ref.1), channel_id=1, source_target_pairs={{0,1},{1,0},{2,3},{3,2},{4,5},{5,4},{6,7},{7,6},{8,9},{9,8},{10,11... | collective-permute-start | bytes 2359304 | tf_op jit(solution)/shard_map/ppermute | solution.py:435
  3.2 1.3 %fusion.2 = (bf16[256,1024]{1,0:T(8,128)(2,1)S(1)}, bf16[256,1024]{1,0:T(8,128)(2,1)S(1)}) fusion(bf16[256,1536]{1,0:T(8,128)(2,1)} %own_ref.1), kind=kLoop, calls=%fused_computation.8 | loop fusion | bytes 2097152 | tf_op jit(solution)/shard_map/slice | solution.py:444
  4.6 8.6 %collective-permute-start.3 = (bf16[256,1024]{1,0:T(8,128)(2,1)S(1)}, bf16[256,1024]{1,0:T(8,128)(2,1)S(1)}, u32[]{:S(2)}, u32[]{:S(2)}) collective-permute-start(bf16[256,1024]{1,0:T(8,128)(2,1)S(1)} %get-tuple-element.18), channel_id=1, source_target_pairs={{0,254},{2,0},{4,2},{6,4},{8,6},{10,8},{12,10},{14,12},{16,14},{18... | collective-permute-start | bytes 1572872 | tf_op jit(solution)/shard_map/ppermute | solution.py:432
  13.2 10.1 %shard_map.118 = (bf16[2,512,4096]{2,1,0:T(8,128)(2,1)}, bf16[1,1024]{1,0:T(2,128)(2,1)}) custom-call(bf16[2,4096,512]{2,1,0:T(8,128)(2,1)} %basis_ref.1), custom_call_target="tpu_custom_call" | custom-call | flops 10000000000 | bytes 16777216 | tf_op jit(solution)/shard_map/pallas_call | solution.py:53
  23.3 0.8 fusion.1
  24.1 1.3 %collective-permute-done.2 = bf16[256,1024]{1,0:T(8,128)(2,1)S(1)} collective-permute-done((bf16[256,1024]{1,0:T(8,128)(2,1)S(1)}, bf16[256,1024]{1,0:T(8,128)(2,1)S(1)}, u32[]{:S(2)}, u32[]{:S(2)}) %collective-permute-start.2) | collective-permute-done | bytes 524320 | tf_op jit(solution)/shard_map/ppermute | solution.py:432
  25.4 0.2 maximum_add_fusion.side_ref
  25.7 0.7 collective-permute-start.4
  26.9 1.8 %collective-permute-done.4.side_sib_ref = bf16[512,1024]{1,0:T(8,128)(2,1)} collective-permute-done((bf16[512,1024]{1,0:T(8,128)(2,1)S(1)}, bf16[512,1024]{1,0:T(8,128)(2,1)}, u32[]{:S(2)}, u32[]{:S(2)}) %collective-permute-start.4) | collective-permute-done | bytes 1048608 | tf_op jit(solution)/shard_map/ppermute | solution.py:435
  28.8 11.4 %shard_map.119 = (bf16[2,256,4096]{2,1,0:T(8,128)(2,1)}, f32[72,128]{1,0:T(8,128)S(1)}) custom-call(s32[10]{0:T(128)S(1)} %pad_add_fusion.scal_ref, bf16[256,1536]{1,0:T(8,128)(2,1)S(1)} %copy-done, bf16[256,1536]{1,0:T(8,128)(2,1)S(1)} %collective-permute-done.1.sib_ref, bf16[512,1024]{1,0:T(8,128)(2,1)} %copy-done.5, ...), custom_call_target="tpu_custom_call" | custom-call | tf_op jit(solution)/shard_map/pallas_call | solution.py:197
  40.3 0.5 collective-permute-start.5
  40.7 0.9 collective-permute-done.5
  41.7 7.0 %collective-permute-start.8 = (f32[72,128]{1,0:T(8,128)S(1)}, f32[72,128]{1,0:T(8,128)S(1)}, u32[]{:S(2)}, u32[]{:S(2)}) collective-permute-start(f32[72,128]{1,0:T(8,128)S(1)} %add.21.x_ref), channel_id=1, source_target_pairs={{0,254},{2,0},{4,2},{6,4},{8,6},{10,8},{12,10},{14,12},{16,14},{18... | collective-permute-start | bytes 110600 | tf_op jit(solution)/shard_map/ppermute | solution.py:432
  48.8 2.3 %collective-permute-start.9 = (f32[72,128]{1,0:T(8,128)S(1)}, f32[72,128]{1,0:T(8,128)S(1)}, u32[]{:S(2)}, u32[]{:S(2)}) collective-permute-start(f32[72,128]{1,0:T(8,128)S(1)} %add.21.x_ref), channel_id=1, source_target_pairs={{0,252},{2,254},{4,0},{6,2},{8,4},{10,6},{12,8},{14,10},{16,12},{1... | collective-permute-start | bytes 110600 | tf_op jit(solution)/shard_map/ppermute | solution.py:432
  51.4 1.7 %collective-permute-done.9.r2_ref = f32[72,128]{1,0:T(8,128)S(1)} collective-permute-done((f32[72,128]{1,0:T(8,128)S(1)}, f32[72,128]{1,0:T(8,128)S(1)}, u32[]{:S(2)}, u32[]{:S(2)}) %collective-permute-start.9) | collective-permute-done | bytes 36896 | tf_op jit(solution)/shard_map/ppermute | solution.py:432
  53.1 11.0 %shard_map.120.mats_ref = bf16[2,512,512]{2,1,0:T(8,128)(2,1)S(1)} custom-call(s32[10]{0:T(128)S(1)} %pad_add_fusion.scal_ref, f32[72,128]{1,0:T(8,128)S(1)} %add.21.x_ref, f32[72,128]{1,0:T(8,128)S(1)} %collective-permute-done.6.l1_ref, f32[72,128]{1,0:T(8,128)S(1)} %collective-permute-done.7.l2_ref, f32[72,128]{1,0:T(8,128)S(1)} %collective-permute-done.8.r1_ref, ...), custom_call_target="tpu_custom_call" | custom-call | tf_op jit(solution)/shard_map/pallas_call | solution.py:303
  64.1 1.9 %collective-permute-start.10 = (bf16[2,512,512]{2,1,0:T(8,128)(2,1)S(1)}, bf16[2,512,512]{2,1,0:T(8,128)(2,1)S(1)}, u32[]{:S(2)}, u32[]{:S(2)}) collective-permute-start(bf16[2,512,512]{2,1,0:T(8,128)(2,1)S(1)} %shard_map.120.mats_ref), channel_id=1, source_target_pairs={{0,1},{1,0},{2,3},{3,2},{4,5},{5,4},{6,7},{7,6},{8,9},{9,8},{10,11... | collective-permute-start | bytes 3145736 | tf_op jit(solution)/shard_map/ppermute | solution.py:435
  66.0 0.3 collective-permute-start
  66.3 2.0 %collective-permute-done.other_ref = s32[10]{0:T(128)S(1)} collective-permute-done((s32[10]{0:T(128)S(1)}, s32[10]{0:T(128)S(1)}, u32[]{:S(2)}, u32[]{:S(2)}) %collective-permute-start) | collective-permute-done | bytes 72 | tf_op jit(solution)/shard_map/ppermute | solution.py:435
  68.3 1.6 %shard_map.122 = (bf16[256,1024]{1,0:T(8,128)(2,1)S(1)}, bf16[256,1024]{1,0:T(8,128)(2,1)S(1)}) custom-call(s32[10]{0:T(128)S(1)} %pad_add_fusion.scal_ref, s32[10]{0:T(128)S(1)} %collective-permute-done.other_ref, bf16[2,512,512]{2,1,0:T(8,128)(2,1)S(1)} %shard_map.120.mats_ref, bf16[2,512,512]{2,1,0:T(8,128)(2,1)S(1)} %collective-permute-done.10.got_ref), custom_call_target="tpu_custom_call" | custom-call | tf_op jit(solution)/shard_map/pallas_call | solution.py:360
  70.0 6.9 %collective-permute-start.12 = (bf16[256,1024]{1,0:T(8,128)(2,1)S(1)}, bf16[256,1024]{1,0:T(8,128)(2,1)S(1)}, u32[]{:S(2)}, u32[]{:S(2)}) collective-permute-start(bf16[256,1024]{1,0:T(8,128)(2,1)S(1)} %get-tuple-element.16), channel_id=1, source_target_pairs={{0,254},{2,0},{4,2},{6,4},{8,6},{10,8},{12,10},{14,12},{16,14},{18... | collective-permute-start | bytes 1572872 | tf_op jit(solution)/shard_map/ppermute | solution.py:432
  76.9 1.3 %shard_map.121.own_ref = f32[256,1536]{1,0:T(8,128)S(1)} custom-call(s32[10]{0:T(128)S(1)} %pad_add_fusion.scal_ref, s32[10]{0:T(128)S(1)} %collective-permute-done.other_ref, bf16[2,512,512]{2,1,0:T(8,128)(2,1)S(1)} %shard_map.120.mats_ref, bf16[2,512,512]{2,1,0:T(8,128)(2,1)S(1)} %collective-permute-done.10.got_ref), custom_call_target="tpu_custom_call" | custom-call | flops 1000000000 | bytes 4194304 | tf_op jit(solution)/shard_map/pallas_call | solution.py:375
  78.2 10.5 %collective-permute-done.11.left_ref = bf16[256,1024]{1,0:T(8,128)(2,1)S(1)} collective-permute-done((bf16[256,1024]{1,0:T(8,128)(2,1)S(1)}, bf16[256,1024]{1,0:T(8,128)(2,1)S(1)}, u32[]{:S(2)}, u32[]{:S(2)}) %collective-permute-start.11) | collective-permute-done | bytes 524320 | tf_op jit(solution)/shard_map/ppermute | solution.py:432
  88.6 1.2 %shard_map.123 = f32[256,1536]{1,0:T(8,128)} custom-call(f32[256,1536]{1,0:T(8,128)S(1)} %shard_map.121.own_ref, bf16[256,1024]{1,0:T(8,128)(2,1)S(1)} %collective-permute-done.11.left_ref, bf16[256,1024]{1,0:T(8,128)(2,1)S(1)} %collective-permute-done.12.right_ref), custom_call_target="tpu_custom_call" | custom-call | tf_op jit(solution)/shard_map/pallas_call | solution.py:403
  (47 shorter events, 1.2 us)
Async XLA Ops:
  0.0 23.3 %collective-permute-start.1 = (bf16[256,1536]{1,0:T(8,128)(2,1)}, bf16[256,1536]{1,0:T(8,128)(2,1)S(1)}, u32[]{:S(2)}, u32[]{:S(2)}) collective-permute-start(bf16[256,1536]{1,0:T(8,128)(2,1)} %own_ref.1), channel_id=1, source_target_pairs={{0,1},{1,0},{2,3},{3,2},{4,5},{5,4},{6,7},{7,6},{8,9},{9,8},{10,11... | collective-permute-start | bytes 2359304 | tf_op jit(solution)/shard_map/ppermute | solution.py:435
  4.5 20.9 %collective-permute-start.2 = (bf16[256,1024]{1,0:T(8,128)(2,1)S(1)}, bf16[256,1024]{1,0:T(8,128)(2,1)S(1)}, u32[]{:S(2)}, u32[]{:S(2)}) collective-permute-start(bf16[256,1024]{1,0:T(8,128)(2,1)S(1)} %get-tuple-element.17), channel_id=1, source_target_pairs={{0,2},{2,4},{4,6},{6,8},{8,10},{10,12},{12,14},{14,16},{16,18},{18... | collective-permute-start | bytes 1572872 | tf_op jit(solution)/shard_map/ppermute | solution.py:432
  4.6 20.8 %collective-permute-start.3 = (bf16[256,1024]{1,0:T(8,128)(2,1)S(1)}, bf16[256,1024]{1,0:T(8,128)(2,1)S(1)}, u32[]{:S(2)}, u32[]{:S(2)}) collective-permute-start(bf16[256,1024]{1,0:T(8,128)(2,1)S(1)} %get-tuple-element.18), channel_id=1, source_target_pairs={{0,254},{2,0},{4,2},{6,4},{8,6},{10,8},{12,10},{14,12},{16,14},{18... | collective-permute-start | bytes 1572872 | tf_op jit(solution)/shard_map/ppermute | solution.py:432
  23.3 3.1 %copy-start.9 = (f32[256]{0:T(256)S(1)}, f32[256]{0:T(256)}, u32[]{:S(2)}) copy-start(f32[256]{0:T(256)} %param.17) | copy-start | bytes 3076
  23.3 3.3 %copy-start.10 = (f32[256]{0:T(256)S(1)}, f32[256]{0:T(256)}, u32[]{:S(2)}) copy-start(f32[256]{0:T(256)} %param.18) | copy-start | bytes 3076
  23.3 3.4 %copy-start.6 = (bf16[256,64]{0,1:T(8,128)(2,1)S(1)}, bf16[256,64]{0,1:T(8,128)(2,1)}, u32[]{:S(2)}) copy-start(bf16[256,64]{0,1:T(8,128)(2,1)} %param.19) | copy-start | bytes 98308
  23.3 5.5 %copy-start = (bf16[256,1536]{1,0:T(8,128)(2,1)S(1)}, bf16[256,1536]{1,0:T(8,128)(2,1)}, u32[]{:S(2)}) copy-start(bf16[256,1536]{1,0:T(8,128)(2,1)} %own_ref.1) | copy-start | bytes 2359300
  23.3 5.4 %copy-start.2 = (f32[2,4096]{1,0:T(2,128)S(1)}, f32[2,4096]{1,0:T(2,128)}, u32[]{:S(2)}) copy-start(f32[2,4096]{1,0:T(2,128)} %w_ref.3) | copy-start | bytes 98308
  23.3 5.4 %copy-start.3 = (s32[2,4096]{1,0:T(2,128)S(1)}, s32[2,4096]{1,0:T(2,128)}, u32[]{:S(2)}) copy-start(s32[2,4096]{1,0:T(2,128)} %atom_ref.3) | copy-start | bytes 98308
  25.6 3.1 %copy-start.5 = (bf16[512,1024]{1,0:T(8,128)(2,1)}, bf16[512,1024]{1,0:T(8,128)(2,1)S(1)}, u32[]{:S(2)}) copy-start(bf16[512,1024]{1,0:T(8,128)(2,1)S(1)} %maximum_add_fusion.side_ref) | copy-start | bytes 3145732
  25.7 3.1 %collective-permute-start.4 = (bf16[512,1024]{1,0:T(8,128)(2,1)S(1)}, bf16[512,1024]{1,0:T(8,128)(2,1)}, u32[]{:S(2)}, u32[]{:S(2)}) collective-permute-start(bf16[512,1024]{1,0:T(8,128)(2,1)S(1)} %maximum_add_fusion.side_ref), channel_id=1, source_target_pairs={{0,1},{1,0},{2,3},{3,2},{4,5},{5,4},{6,7},{7,6},{8,9},{9,8},{10,11... | collective-permute-start | bytes 3145736 | tf_op jit(solution)/shard_map/ppermute | solution.py:435
  28.8 22.3 %copy-start.11 = (bf16[256]{0:T(256)(128)(2,1)S(1)}, bf16[256]{0:T(256)(128)(2,1)}, u32[]{:S(2)}) copy-start(bf16[256]{0:T(256)(128)(2,1)} %param.23) | copy-start | bytes 1540
  28.8 22.4 %copy-start.7 = (f32[256]{0:T(256)S(1)}, f32[256]{0:T(256)}, u32[]{:S(2)}) copy-start(f32[256]{0:T(256)} %param.22) | copy-start | bytes 3076
  28.8 24.3 %copy-start.1 = (bf16[256,256]{1,0:T(8,128)(2,1)S(1)}, bf16[256,256]{1,0:T(8,128)(2,1)}, u32[]{:S(2)}) copy-start(bf16[256,256]{1,0:T(8,128)(2,1)} %hw_ref.1) | copy-start | bytes 393220
  28.8 24.3 %copy-start.4 = (bf16[64,256]{1,0:T(8,128)(2,1)S(1)}, bf16[64,256]{1,0:T(8,128)(2,1)}, u32[]{:S(2)}) copy-start(bf16[64,256]{1,0:T(8,128)(2,1)} %atom_in_ref.1) | copy-start | bytes 98308
  40.3 1.3 %collective-permute-start.5 = (f32[72,128]{1,0:T(8,128)S(1)}, f32[72,128]{1,0:T(8,128)S(1)}, u32[]{:S(2)}, u32[]{:S(2)}) collective-permute-start(f32[72,128]{1,0:T(8,128)S(1)} %get-tuple-element.13), channel_id=1, source_target_pairs={{0,1},{1,0},{2,3},{3,2},{4,5},{5,4},{6,7},{7,6},{8,9},{9,8},{10,11... | collective-permute-start | bytes 110600 | tf_op jit(solution)/shard_map/ppermute | solution.py:435
  41.6 9.7 %collective-permute-start.6 = (f32[72,128]{1,0:T(8,128)S(1)}, f32[72,128]{1,0:T(8,128)S(1)}, u32[]{:S(2)}, u32[]{:S(2)}) collective-permute-start(f32[72,128]{1,0:T(8,128)S(1)} %add.21.x_ref), channel_id=1, source_target_pairs={{0,2},{2,4},{4,6},{6,8},{8,10},{10,12},{12,14},{14,16},{16,18},{18... | collective-permute-start | bytes 110600 | tf_op jit(solution)/shard_map/ppermute | solution.py:432
  41.6 9.7 %collective-permute-start.7 = (f32[72,128]{1,0:T(8,128)S(1)}, f32[72,128]{1,0:T(8,128)S(1)}, u32[]{:S(2)}, u32[]{:S(2)}) collective-permute-start(f32[72,128]{1,0:T(8,128)S(1)} %add.21.x_ref), channel_id=1, source_target_pairs={{0,4},{2,6},{4,8},{6,10},{8,12},{10,14},{12,16},{14,18},{16,20},{1... | collective-permute-start | bytes 110600 | tf_op jit(solution)/shard_map/ppermute | solution.py:432
  41.7 9.6 %collective-permute-start.8 = (f32[72,128]{1,0:T(8,128)S(1)}, f32[72,128]{1,0:T(8,128)S(1)}, u32[]{:S(2)}, u32[]{:S(2)}) collective-permute-start(f32[72,128]{1,0:T(8,128)S(1)} %add.21.x_ref), channel_id=1, source_target_pairs={{0,254},{2,0},{4,2},{6,4},{8,6},{10,8},{12,10},{14,12},{16,14},{18... | collective-permute-start | bytes 110600 | tf_op jit(solution)/shard_map/ppermute | solution.py:432
  48.8 4.3 %collective-permute-start.9 = (f32[72,128]{1,0:T(8,128)S(1)}, f32[72,128]{1,0:T(8,128)S(1)}, u32[]{:S(2)}, u32[]{:S(2)}) collective-permute-start(f32[72,128]{1,0:T(8,128)S(1)} %add.21.x_ref), channel_id=1, source_target_pairs={{0,252},{2,254},{4,0},{6,2},{8,4},{10,6},{12,8},{14,10},{16,12},{1... | collective-permute-start | bytes 110600 | tf_op jit(solution)/shard_map/ppermute | solution.py:432
  64.1 4.2 %collective-permute-start.10 = (bf16[2,512,512]{2,1,0:T(8,128)(2,1)S(1)}, bf16[2,512,512]{2,1,0:T(8,128)(2,1)S(1)}, u32[]{:S(2)}, u32[]{:S(2)}) collective-permute-start(bf16[2,512,512]{2,1,0:T(8,128)(2,1)S(1)} %shard_map.120.mats_ref), channel_id=1, source_target_pairs={{0,1},{1,0},{2,3},{3,2},{4,5},{5,4},{6,7},{7,6},{8,9},{9,8},{10,11... | collective-permute-start | bytes 3145736 | tf_op jit(solution)/shard_map/ppermute | solution.py:435
  66.0 2.3 %collective-permute-start = (s32[10]{0:T(128)S(1)}, s32[10]{0:T(128)S(1)}, u32[]{:S(2)}, u32[]{:S(2)}) collective-permute-start(s32[10]{0:T(128)S(1)} %pad_add_fusion.scal_ref), channel_id=1, source_target_pairs={{0,1},{1,0},{2,3},{3,2},{4,5},{5,4},{6,7},{7,6},{8,9},{9,8},{10,11... | collective-permute-start | bytes 128 | tf_op jit(solution)/shard_map/ppermute | solution.py:435
  69.9 18.7 %collective-permute-start.11 = (bf16[256,1024]{1,0:T(8,128)(2,1)S(1)}, bf16[256,1024]{1,0:T(8,128)(2,1)S(1)}, u32[]{:S(2)}, u32[]{:S(2)}) collective-permute-start(bf16[256,1024]{1,0:T(8,128)(2,1)S(1)} %get-tuple-element.15), channel_id=1, source_target_pairs={{0,2},{2,4},{4,6},{6,8},{8,10},{10,12},{12,14},{14,16},{16,18},{18... | collective-permute-start | bytes 1572872 | tf_op jit(solution)/shard_map/ppermute | solution.py:432
  70.0 18.6 %collective-permute-start.12 = (bf16[256,1024]{1,0:T(8,128)(2,1)S(1)}, bf16[256,1024]{1,0:T(8,128)(2,1)S(1)}, u32[]{:S(2)}, u32[]{:S(2)}) collective-permute-start(bf16[256,1024]{1,0:T(8,128)(2,1)S(1)} %get-tuple-element.16), channel_id=1, source_target_pairs={{0,254},{2,0},{4,2},{6,4},{8,6},{10,8},{12,10},{14,12},{16,14},{18... | collective-permute-start | bytes 1572872 | tf_op jit(solution)/shard_map/ppermute | solution.py:432
  (1 other events, 3.1 us)
